TPU v7x, 128 devices: a whole 4x4x4 slice. The times are simulated.
128 devices in a mesh: dp: 2 (over core), context: 16 (over x, z), tensor: 4 (over y).
Axes of the slice: x: 4, y: 4, z: 4, core: 2. Of those that a mesh axis runs over, the one named last changes fastest.
Arguments:
- token_ids: int32 [24576], P(('dp', 'context')), parts along dimension 0, may hold values from 0 to 511
- subst_pos: int32 [1536], P(('dp', 'context')), parts along dimension 0, may hold values from 0 to 767, as said below
- subst_base: int32 [1536], P(('dp', 'context')), parts along dimension 0, may hold values from 0 to 511
- window_lengths: int32 [64], P('dp'), parts along dimension 0, may hold values from 1 to 768, 12288 in all
- embed_table: bfloat16 [512, 4096], replicated, may hold values from -6 to 6
- norm_gain: float32 [4096], replicated, may hold values from 0.5 to 1.5
- in_weight: bfloat16 [4096, 3, 4096], P('context', None, 'tensor'), may hold values from -0.09375 to 0.09375
- short_filter: float32 [3, 3, 4096], P(None, None, 'tensor'), may hold values from -4 to 4
- mr_filter: float32 [128, 4096], P(None, 'tensor'), may hold values from -0.5 to 0.5
- mr_decay: float32 [4096], P('tensor'), may hold values from 0.002 to 0.08
- out_weight: bfloat16 [4096, 4096], P('context', 'tensor'), may hold values from -0.09375 to 0.09375
Outputs:
- block_out: bfloat16 [24576, 4096], P(('dp', 'context'), 'tensor'), parts along dimension 0
There are 2 independent parts, one for each index of `dp`. A program takes and returns all parts, laid end to end along the dimension named above; an argument that names none is the same for every part. Nothing has to cross between parts.
Inputs may be any that keep to these rules, and one draw needn't show every extreme that they name: `subst_pos`: the j-th substitution of a shard lies in that shard's rows j * 16 to (j + 1) * 16 - 1; each shard's first substitution is at row 0 and its last at row 767. `window_lengths`: the lengths sum to 12288.
All inputs are finite; a program needn't handle non-finite values.
Results may differ from a plain program's by a relative error of at most 0.0085.
Values may be sent and summed in bfloat16 or wider, within the bound.
A program may use at most 320 MiB of HBM per device.

v0:
```python
import jax
import jax.numpy as jnp
from jax import lax
from jax.sharding import PartitionSpec as P


def passed_along(value, axis, steps):
    count = lax.axis_size(axis)
    first, last = (max(0, -steps), min(count, count - steps))
    return lax.ppermute(value, axis, [(source, source + steps) for source in range(first, last)])


def window_age(window_lengths, first_row, row_count):
    starts = jnp.cumsum(window_lengths) - window_lengths
    positions = first_row + jnp.arange(row_count, dtype=jnp.int32)
    matches = starts[None, :] <= positions[:, None]
    doc_begin = jnp.max(jnp.where(matches, starts[None, :], -1), axis=1)
    return jnp.where(doc_begin >= 0, positions - doc_begin, -1)


def short_mix(extended, filters, row_age):
    out_rows = extended.shape[0] - 2
    result = jnp.zeros((out_rows,) + extended.shape[1:], jnp.float32)
    for tap_index in range(3):
        keep = (tap_index <= row_age).astype(jnp.float32)[:, None, None]
        window = extended[2 - tap_index : 2 - tap_index + out_rows].astype(jnp.float32)
        result = result + filters[tap_index][None] * window * keep
    return result


def long_mix(extended, tap_table, row_age):
    tap_count = tap_table.shape[0]
    out_rows = extended.shape[0] - (tap_count - 1)
    result = jnp.zeros((out_rows, extended.shape[1]), jnp.float32)
    for tap_index in range(tap_count):
        keep = (tap_index <= row_age).astype(jnp.float32)[:, None]
        begin_row = tap_count - 1 - tap_index
        window = extended[begin_row : begin_row + out_rows].astype(jnp.float32)
        result = result + tap_table[tap_index][None, :] * window * keep
    return result


def body(
    token_ids,
    subst_pos,
    subst_base,
    window_lengths,
    embed_table,
    norm_gain,
    in_weight,
    short_filter,
    mr_filter,
    mr_decay,
    out_weight,
):
    row_count = token_ids.shape[0]
    channels = in_weight.shape[2]
    tap_count = mr_filter.shape[0]
    rim_rows = tap_count - 1
    matches = subst_pos[:, None] == jnp.arange(row_count, dtype=jnp.int32)[None, :]
    chosen = jnp.sum(jnp.where(matches, subst_base[:, None], 0), axis=0)
    touched = jnp.any(matches, axis=0)
    new_ids = jnp.where(touched, chosen, token_ids)
    embedded = jnp.take(embed_table, new_ids, axis=0)
    x_wide = embedded.astype(jnp.float32)
    scale = lax.rsqrt(jnp.mean(x_wide * x_wide, axis=1, keepdims=True) + 1e-06)
    normed = (x_wide * scale * norm_gain[None, :]).astype(jnp.bfloat16)
    first_row = lax.axis_index("context") * row_count
    row_age = window_age(window_lengths, first_row, row_count)
    weight_rows = lax.all_gather(in_weight, "context", axis=0, tiled=True)
    columns = normed
    flat_rows = weight_rows.reshape(weight_rows.shape[0], -1)
    totals = jnp.dot(columns, flat_rows, preferred_element_type=jnp.float32)
    projected_in = totals.astype(jnp.bfloat16).reshape(row_count, 3, channels)
    query_in = projected_in[:, 0, :]
    pair_in = projected_in[:, 1:, :]
    pair_rim = passed_along(pair_in[row_count - 2 :], "context", 1)
    pair_ext = jnp.concatenate([pair_rim, pair_in], axis=0)
    pair_out = short_mix(pair_ext, short_filter[:, 1:, :], row_age)
    product = (pair_out[:, 0, :] * pair_out[:, 1, :]).astype(jnp.bfloat16)
    product_rim = passed_along(product[row_count - rim_rows :], "context", 1)
    product_ext = jnp.concatenate([product_rim, product], axis=0)
    query_rim = passed_along(query_in[row_count - 2 :], "context", 1)
    query_ext = jnp.concatenate([query_rim, query_in], axis=0)[:, None, :]
    query_out = short_mix(query_ext, short_filter[:, 0:1, :], row_age)[:, 0, :]
    tap_table = mr_filter * jnp.exp(
        -mr_decay[None, :] * jnp.arange(tap_count, dtype=jnp.float32)[:, None]
    )
    long_out = long_mix(product_ext, tap_table, row_age)
    gated_out = (query_out * long_out).astype(jnp.bfloat16)
    features = lax.all_gather(gated_out, "tensor", axis=1, tiled=True)
    weight_rows = lax.all_gather(out_weight, "context", axis=0, tiled=True)
    columns = lax.slice_in_dim(features, 0, weight_rows.shape[0], axis=1)
    projected = jnp.zeros((row_count, out_weight.shape[1]), jnp.float32) + jnp.dot(
        columns, weight_rows, preferred_element_type=jnp.float32
    )
    residual = lax.dynamic_slice_in_dim(
        embedded, lax.axis_index("tensor") * out_weight.shape[1], out_weight.shape[1], 1
    ).astype(jnp.float32)
    return (residual + projected).astype(jnp.bfloat16)


def solution(mesh):
    in_specs = (
        P(("dp", "context")),
        P(("dp", "context")),
        P(("dp", "context")),
        P("dp"),
        P(),
        P(),
        P("context", None, "tensor"),
        P(None, None, "tensor"),
        P(None, "tensor"),
        P("tensor"),
        P("context", "tensor"),
    )
    out_specs = P(("dp", "context"), "tensor")
    return jax.shard_map(body, mesh=mesh, in_specs=in_specs, out_specs=out_specs, check_vma=False)
```

profile of v0, /device:TPU:0, one launch (start us, length us, event | category | flops | bytes accessed | tf_op | source)
XLA Modules:
  0.0 541.1 jit_solution(13420415401367187604)
XLA Ops:
  6.6 2.6 copy.23
  9.3 0.7 all-gather.8.cloned.1.call-update
  10.2 0.7 fusion.145
  10.9 0.7 fusion.144
  11.6 0.7 fusion.146
  12.2 0.7 fusion.142
  12.9 0.7 fusion.141
  13.6 0.7 fusion.140
  14.3 0.7 fusion.143
  15.0 0.6 fusion.147
  16.0 0.6 compare_convert_fusion.83
  16.6 1.0 compare_convert_fusion.82
  17.8 14.7 %gather_fusion = bf16[768,4096]{1,0:T(8,128)(2,1)} fusion(bf16[512,4096]{1,0:T(8,128)(2,1)} %param.15, s32[1024]{0:T(1024)S(1)} %pad_clamp_fusion), kind=kCustom, calls=%fused_computation | custom fusion | bytes 12585984 | tf_op jit(solution)/shard_map/jit(_take)/gather | solution.py:64
  32.5 7.4 %fusion = (f32[768]{0:T(1024)S(1)}, bf16[768,4096]{1,0:T(8,128)(2,1)}) fusion(bf16[768,4096]{1,0:T(8,128)(2,1)} %gather_fusion, pred[768]{0:T(1024)(128)(4,1)S(1)} %get-tuple-element.9), kind=kLoop, calls=%fused_computation.129 | loop fusion | flops 12582144 | bytes 12586752 | tf_op jit(solution)/shard_map/reduce_sum | solution.py:66
  39.9 135.9 %all-gather.4.cloned.1.call-done = bf16[4096,3,1024]{0,2,1:T(8,128)(2,1)} async-done(((bf16[256,3,1024]{0,2,1:T(8,128)(2,1)}), bf16[4096,3,1024]{0,2,1:T(8,128)(2,1)}) %all-gather.4.cloned.1.call-update) | async-done | bytes 25165840 | tf_op jit(solution)/shard_map/all_gather | solution.py:70
  175.9 26.1 %fusion.7 = bf16[768,3072]{1,0:T(8,128)(2,1)} fusion(bf16[4096,3072]{0,1:T(8,128)(2,1)} %bitcast.290, bf16[768,4096]{1,0:T(8,128)(2,1)} %get-tuple-element.8, f32[4096]{0:T(1024)S(1)} %copy-done.9, f32[768]{0:T(1024)S(1)} %add_rsqrt_fusion), kind=kOutput, calls=%fused_computation.137 | convolution fusion | flops 19342295040 | bytes 36195328 | tf_op jit(solution)/shard_map/dot_general | solution.py:73
  202.0 6.7 %copy.24 = bf16[768,3072]{0,1:T(8,128)(2,1)} copy(bf16[768,3072]{1,0:T(8,128)(2,1)} %fusion.7) | data formatting | bytes 9437184 | tf_op jit(solution)/shard_map/convert_element_type | solution.py:74
  208.6 1.4 slice.1118
  210.0 2.4 slice_bitcast_fusion
  212.5 2.5 collective-permute-start.1
  215.0 1.8 slice_bitcast_fusion.2
  216.8 0.2 slice.1117
  217.0 2.9 collective-permute-start
  219.9 18.6 %collective-permute-done.1 = bf16[2,2,1024]{0,2,1:T(8,128)(2,1)S(1)} collective-permute-done((bf16[2,2,1024]{0,2,1:T(8,128)(2,1)S(1)}, bf16[2,2,1024]{0,2,1:T(8,128)(2,1)S(1)}, u32[]{:S(2)}, u32[]{:S(2)}) %collective-permute-start.1) | collective-permute-done | bytes 8224 | tf_op jit(solution)/shard_map/ppermute | solution.py:10
  238.5 4.3 multiply_add_fusion
  242.8 0.3 fusion.11
  243.3 4.4 collective-permute-start.2
  247.7 0.3 fusion.151
  248.0 12.2 %collective-permute-done.2 = bf16[127,1024]{0,1:T(8,128)(2,1)S(1)} collective-permute-done((bf16[127,1024]{0,1:T(8,128)(2,1)S(1)}, bf16[127,1024]{0,1:T(8,128)(2,1)S(1)}, u32[]{:S(2)}, u32[]{:S(2)}) %collective-permute-start.2) | collective-permute-done | bytes 260128 | tf_op jit(solution)/shard_map/ppermute | solution.py:10
  260.2 5.7 %fusion.57 = (bf16[768,1024]{0,1:T(8,128)(2,1)}, bf16[768,1024]{0,1:T(8,128)(2,1)}, bf16[768,1024]{0,1:T(8,128)(2,1)}, bf16[768,1024]{0,1:T(8,128)(2,1)}, bf16[7...) fusion(bf16[127,1024]{0,1:T(8,128)(2,1)S(1)} %collective-permute-done.2, bf16[768,1024]{0,1:T(8,128)(2,1)S(1)} %fusion.151), kind=kLoop, calls=%fused_computation.196 | loop fusion | flops 18874368 | bytes 11270144 | tf_op jit(solution)/shard_map/concatenate | solution.py:82
  266.0 5.7 %fusion.63 = (bf16[768,1024]{0,1:T(8,128)(2,1)}, bf16[768,1024]{0,1:T(8,128)(2,1)}, bf16[768,1024]{0,1:T(8,128)(2,1)}, bf16[768,1024]{0,1:T(8,128)(2,1)}, bf16[7...) fusion(bf16[127,1024]{0,1:T(8,128)(2,1)S(1)} %collective-permute-done.2, bf16[768,1024]{0,1:T(8,128)(2,1)S(1)} %fusion.151), kind=kLoop, calls=%fused_computation.202 | loop fusion | flops 18874368 | bytes 11270144 | tf_op jit(solution)/shard_map/concatenate | solution.py:82
  271.7 5.7 %fusion.69 = (bf16[768,1024]{0,1:T(8,128)(2,1)}, bf16[768,1024]{0,1:T(8,128)(2,1)}, bf16[768,1024]{0,1:T(8,128)(2,1)}, bf16[768,1024]{0,1:T(8,128)(2,1)}, bf16[7...) fusion(bf16[127,1024]{0,1:T(8,128)(2,1)S(1)} %collective-permute-done.2, bf16[768,1024]{0,1:T(8,128)(2,1)S(1)} %fusion.151), kind=kLoop, calls=%fused_computation.208 | loop fusion | flops 18874368 | bytes 11270144 | tf_op jit(solution)/shard_map/concatenate | solution.py:82
  277.4 5.7 %fusion.75 = (bf16[768,1024]{0,1:T(8,128)(2,1)}, bf16[768,1024]{0,1:T(8,128)(2,1)}, bf16[768,1024]{0,1:T(8,128)(2,1)}, bf16[768,1024]{0,1:T(8,128)(2,1)}, bf16[7...) fusion(bf16[127,1024]{0,1:T(8,128)(2,1)S(1)} %collective-permute-done.2, bf16[768,1024]{0,1:T(8,128)(2,1)S(1)} %fusion.151), kind=kLoop, calls=%fused_computation.214 | loop fusion | flops 18874368 | bytes 11270144 | tf_op jit(solution)/shard_map/concatenate | solution.py:82
  283.2 5.7 %fusion.81 = (bf16[768,1024]{0,1:T(8,128)(2,1)}, bf16[768,1024]{0,1:T(8,128)(2,1)}, bf16[768,1024]{0,1:T(8,128)(2,1)}, bf16[768,1024]{0,1:T(8,128)(2,1)}, bf16[7...) fusion(bf16[127,1024]{0,1:T(8,128)(2,1)S(1)} %collective-permute-done.2, bf16[768,1024]{0,1:T(8,128)(2,1)S(1)} %fusion.151), kind=kLoop, calls=%fused_computation.220 | loop fusion | flops 18874368 | bytes 11270144 | tf_op jit(solution)/shard_map/concatenate | solution.py:82
  288.9 5.7 %fusion.87 = (bf16[768,1024]{0,1:T(8,128)(2,1)}, bf16[768,1024]{0,1:T(8,128)(2,1)}, bf16[768,1024]{0,1:T(8,128)(2,1)}, bf16[768,1024]{0,1:T(8,128)(2,1)}, bf16[7...) fusion(bf16[127,1024]{0,1:T(8,128)(2,1)S(1)} %collective-permute-done.2, bf16[768,1024]{0,1:T(8,128)(2,1)S(1)} %fusion.151), kind=kLoop, calls=%fused_computation.226 | loop fusion | flops 18874368 | bytes 11270144 | tf_op jit(solution)/shard_map/concatenate | solution.py:82
  294.6 5.8 %fusion.93 = (bf16[768,1024]{0,1:T(8,128)(2,1)}, bf16[768,1024]{0,1:T(8,128)(2,1)}, bf16[768,1024]{0,1:T(8,128)(2,1)}, bf16[768,1024]{0,1:T(8,128)(2,1)}, bf16[7...) fusion(bf16[127,1024]{0,1:T(8,128)(2,1)S(1)} %collective-permute-done.2, bf16[768,1024]{0,1:T(8,128)(2,1)S(1)} %fusion.151), kind=kLoop, calls=%fused_computation.232 | loop fusion | flops 18874368 | bytes 11270144 | tf_op jit(solution)/shard_map/concatenate | solution.py:82
  300.4 5.8 %fusion.99 = (bf16[768,1024]{0,1:T(8,128)(2,1)}, bf16[768,1024]{0,1:T(8,128)(2,1)}, bf16[768,1024]{0,1:T(8,128)(2,1)}, bf16[768,1024]{0,1:T(8,128)(2,1)}, bf16[7...) fusion(bf16[127,1024]{0,1:T(8,128)(2,1)S(1)} %collective-permute-done.2, bf16[768,1024]{0,1:T(8,128)(2,1)S(1)} %fusion.151), kind=kLoop, calls=%fused_computation.238 | loop fusion | flops 18874368 | bytes 11270144 | tf_op jit(solution)/shard_map/concatenate | solution.py:82
  306.3 5.8 %fusion.105 = (bf16[768,1024]{0,1:T(8,128)(2,1)}, bf16[768,1024]{0,1:T(8,128)(2,1)}, bf16[768,1024]{0,1:T(8,128)(2,1)}, bf16[768,1024]{0,1:T(8,128)(2,1)}, bf16[...) fusion(bf16[127,1024]{0,1:T(8,128)(2,1)S(1)} %collective-permute-done.2, bf16[768,1024]{0,1:T(8,128)(2,1)S(1)} %fusion.151), kind=kLoop, calls=%fused_computation.244 | loop fusion | flops 18874368 | bytes 11270144 | tf_op jit(solution)/shard_map/concatenate | solution.py:82
  312.0 5.9 %fusion.111 = (bf16[768,1024]{0,1:T(8,128)(2,1)}, bf16[768,1024]{0,1:T(8,128)(2,1)}, bf16[768,1024]{0,1:T(8,128)(2,1)}, bf16[768,1024]{0,1:T(8,128)(2,1)}, bf16[...) fusion(bf16[127,1024]{0,1:T(8,128)(2,1)S(1)} %collective-permute-done.2, bf16[768,1024]{0,1:T(8,128)(2,1)S(1)} %fusion.151), kind=kLoop, calls=%fused_computation.250 | loop fusion | flops 18874368 | bytes 11270144 | tf_op jit(solution)/shard_map/concatenate | solution.py:82
  318.0 5.8 %fusion.117 = (bf16[768,1024]{0,1:T(8,128)(2,1)}, bf16[768,1024]{0,1:T(8,128)(2,1)}, bf16[768,1024]{0,1:T(8,128)(2,1)}, bf16[768,1024]{0,1:T(8,128)(2,1)}, bf16[...) fusion(bf16[127,1024]{0,1:T(8,128)(2,1)S(1)} %collective-permute-done.2, bf16[768,1024]{0,1:T(8,128)(2,1)S(1)} %fusion.151), kind=kLoop, calls=%fused_computation.256 | loop fusion | flops 18874368 | bytes 11270144 | tf_op jit(solution)/shard_map/concatenate | solution.py:82
  323.8 5.8 %fusion.123 = (bf16[768,1024]{0,1:T(8,128)(2,1)}, bf16[768,1024]{0,1:T(8,128)(2,1)}, bf16[768,1024]{0,1:T(8,128)(2,1)}, bf16[768,1024]{0,1:T(8,128)(2,1)}, bf16[...) fusion(bf16[127,1024]{0,1:T(8,128)(2,1)S(1)} %collective-permute-done.2, bf16[768,1024]{0,1:T(8,128)(2,1)S(1)} %fusion.151), kind=kLoop, calls=%fused_computation.262 | loop fusion | flops 18874368 | bytes 11270144 | tf_op jit(solution)/shard_map/concatenate | solution.py:82
  329.6 5.8 %fusion.129 = (bf16[768,1024]{0,1:T(8,128)(2,1)}, bf16[768,1024]{0,1:T(8,128)(2,1)}, bf16[768,1024]{0,1:T(8,128)(2,1)}, bf16[768,1024]{0,1:T(8,128)(2,1)}, bf16[...) fusion(bf16[127,1024]{0,1:T(8,128)(2,1)S(1)} %collective-permute-done.2, bf16[768,1024]{0,1:T(8,128)(2,1)S(1)} %fusion.151), kind=kLoop, calls=%fused_computation.268 | loop fusion | flops 18874368 | bytes 11270144 | tf_op jit(solution)/shard_map/concatenate | solution.py:82
  335.4 5.5 %fusion.135 = (bf16[768,1024]{0,1:T(8,128)(2,1)}, bf16[768,1024]{0,1:T(8,128)(2,1)}, bf16[768,1024]{0,1:T(8,128)(2,1)}, bf16[768,1024]{0,1:T(8,128)(2,1)}, bf16[...) fusion(bf16[127,1024]{0,1:T(8,128)(2,1)S(1)} %collective-permute-done.2, bf16[768,1024]{0,1:T(8,128)(2,1)S(1)} %fusion.151), kind=kLoop, calls=%fused_computation.274 | loop fusion | flops 18874368 | bytes 11270144 | tf_op jit(solution)/shard_map/concatenate | solution.py:82
  340.9 44.0 %multiply_add_fusion.1 = f32[768,1024]{0,1:T(8,128)} fusion(bf16[127,1024]{0,1:T(8,128)(2,1)S(1)} %collective-permute-done.2, f32[768]{0:T(1024)} %get-tuple-element.313, f32[1024]{0:T(1024)} %bitcast.264, f32[768]{0:T(1024)} %get-tuple-element.314, f32[1024]{0:T(1024)} %bitcast.265, f32[768]{0:T(1024)} %get-tuple-element.315, f32[1024]{0:T(1024)} %bitcast.266, ...), kind=kLoop, calls=%fused_computation.147 | loop fusion | flops 235143168 | bytes 11578368 | tf_op jit(solution)/shard_map/add | solution.py:39
  384.9 3.4 multiply_multiply_fusion
  388.3 65.2 %multiply_convert_fusion = bf16[768,1024]{0,1:T(8,128)(2,1)} fusion(bf16[768,1024]{0,1:T(8,128)(2,1)} %get-tuple-element.93, bf16[768,1024]{0,1:T(8,128)(2,1)} %get-tuple-element.94, bf16[768,1024]{0,1:T(8,128)(2,1)} %get-tuple-element.92, bf16[768,1024]{0,1:T(8,128)(2,1)} %get-tuple-element.91, bf16[768,1024]{0,1:T(8,128)(2,1)} %get-tuple-element.90, ...), kind=kLoop, calls=%fused_computation.145 | loop fusion | flops 279969792 | bytes 142185472 | tf_op jit(solution)/shard_map/convert_element_type | solution.py:90
  453.5 68.3 %all-gather.6.cloned.1.call-done = bf16[768,4096]{0,1:T(8,128)(2,1)} async-done(((bf16[768,1024]{0,1:T(8,128)(2,1)}), bf16[768,4096]{0,1:T(8,128)(2,1)}) %all-gather.6.cloned.1.call-update) | async-done | bytes 6291472 | tf_op jit(solution)/shard_map/all_gather | solution.py:91
  521.8 12.3 %add_convert_fusion = bf16[768,1024]{1,0:T(8,128)(2,1)} fusion(bf16[768,4096]{0,1:T(8,128)(2,1)} %all-gather.6.cloned.1.call-done, bf16[4096,1024]{1,0:T(8,128)(2,1)} %all-gather.8.cloned.1.call-done, bf16[768,4096]{1,0:T(8,128)(2,1)} %get-tuple-element.8, s32[]{:T(128)S(6)} %select_n.425), kind=kOutput, calls=%fused_computation.144 | convolution fusion | flops 6444810240 | bytes 17825796 | tf_op jit(solution)/shard_map/dot_general | solution.py:94
  (42 shorter events, 1.1 us)
Async XLA Ops:
  6.5 3.5 copy-start.5
  6.5 3.5 copy-start.2
  6.5 8.4 %copy-start.3 = (f32[3,3,1024]{2,1,0:T(4,128)S(1)}, f32[3,3,1024]{2,1,0:T(4,128)}, u32[]{:S(2)}) copy-start(f32[3,3,1024]{2,1,0:T(4,128)} %param.18) | copy-start | bytes 110596
  6.5 9.1 %copy-start.6 = (s32[32]{0:T(128)S(1)}, s32[32]{0:T(128)}, u32[]{:S(2)}) copy-start(s32[32]{0:T(128)} %param.14) | copy-start | bytes 388
  6.5 169.3 %all-gather.4.cloned.1.call-start = ((), (), s32[]{:S(2)}) async-start(), calls=%async_computation | async-start | bytes 26738688 | tf_op jit(solution)/shard_map/all_gather | solution.py:70
  9.2 8.4 %copy-start.7 = (s32[48]{0:T(128)S(1)}, s32[48]{0:T(128)}, u32[]{:S(2)}) copy-start(s32[48]{0:T(128)} %param.12) | copy-start | bytes 580
  9.2 8.5 %copy-start.8 = (s32[48]{0:T(128)S(1)}, s32[48]{0:T(128)}, u32[]{:S(2)}) copy-start(s32[48]{0:T(128)} %param.13) | copy-start | bytes 580
  9.2 8.6 %copy-start.4 = (s32[768]{0:T(1024)S(1)}, s32[768]{0:T(1024)}, u32[]{:S(2)}) copy-start(s32[768]{0:T(1024)} %param.11) | copy-start | bytes 9220
  9.2 444.3 %all-gather.8.cloned.1.call-start = ((), (), s32[]{:S(2)}) async-start(), calls=%async_computation.2 | async-start | bytes 8912896 | tf_op jit(solution)/shard_map/all_gather | solution.py:92
  10.0 511.8 %all-gather.6.cloned.1.call-start = ((), (), s32[]{:S(2)}) async-start(), calls=%async_computation.1 | async-start | bytes 7864320 | tf_op jit(solution)/shard_map/all_gather | solution.py:91
  32.5 143.4 %copy-start.9 = (f32[4096]{0:T(1024)S(1)}, f32[4096]{0:T(1024)}, u32[]{:S(2)}) copy-start(f32[4096]{0:T(1024)} %param.16) | copy-start | bytes 49156
  208.6 8.2 %copy-start.1 = (bf16[768,3072]{0,1:T(8,128)(2,1)S(1)}, bf16[768,3072]{0,1:T(8,128)(2,1)}, u32[]{:S(2)}) copy-start(bf16[768,3072]{0,1:T(8,128)(2,1)} %copy.24) | copy-start | bytes 14155780
  212.5 26.0 %collective-permute-start.1 = (bf16[2,2,1024]{0,2,1:T(8,128)(2,1)S(1)}, bf16[2,2,1024]{0,2,1:T(8,128)(2,1)S(1)}, u32[]{:S(2)}, u32[]{:S(2)}) collective-permute-start(bf16[2,2,1024]{0,2,1:T(8,128)(2,1)S(1)} %slice.1118), channel_id=1, source_target_pairs={{0,4},{4,8},{8,12},{12,16},{16,20},{20,24},{24,28},{28,32},{32,36}... | collective-permute-start | bytes 24584 | tf_op jit(solution)/shard_map/ppermute | solution.py:10
  217.0 171.3 %collective-permute-start = (bf16[2,1024]{0,1:T(8,128)(2,1)}, bf16[2,1024]{0,1:T(8,128)(2,1)}, u32[]{:S(2)}, u32[]{:S(2)}) collective-permute-start(bf16[2,1024]{0,1:T(8,128)(2,1)} %slice_bitcast_fusion.2), channel_id=1, source_target_pairs={{0,4},{4,8},{8,12},{12,16},{16,20},{20,24},{24,28},{28,32},{32,36}... | collective-permute-start | bytes 12296 | tf_op jit(solution)/shard_map/ppermute | solution.py:10
  242.8 4.9 copy-start
  243.3 17.0 %collective-permute-start.2 = (bf16[127,1024]{0,1:T(8,128)(2,1)S(1)}, bf16[127,1024]{0,1:T(8,128)(2,1)S(1)}, u32[]{:S(2)}, u32[]{:S(2)}) collective-permute-start(bf16[127,1024]{0,1:T(8,128)(2,1)S(1)} %slice_bitcast_fusion.1), channel_id=1, source_target_pairs={{0,4},{4,8},{8,12},{12,16},{16,20},{20,24},{24,28},{28,32},{32,36}... | collective-permute-start | bytes 780296 | tf_op jit(solution)/shard_map/ppermute | solution.py:10
Sparse Core Ops, SparseCore 0:
  9.5 166.3 all-gather.3
  178.0 88.6 all-gather.7
  453.6 68.1 all-gather.5
where the time goes:
time: 551 us; the launch traced here: 541 us
  waiting for transfers between devices  236 us (43%)
  other arithmetic  208 us (38%)
  matrix products  38.4 us (7%)
  local copies, waits for them, and re-layouts  35.4 us (6%)
  between operations  13.8 us (3%)
  starting transfers between devices  9.91 us (2%)
    all_gather x1, waiting for transfers between devices, body(): weight_rows = lax.all_gather(in_weight, 'context', axis=0, tiled=True)  136 us
    concatenate x14, other arithmetic, body(): product_ext = jnp.concatenate([product_rim, product], axis=0)  80.7 us
    all_gather x1, waiting for transfers between devices, body(): features = lax.all_gather(gated_out, 'tensor', axis=1, tiled=True)  68.3 us
    convert_element_type x1, other arithmetic, body(): gated_out = (query_out * long_out).astype(jnp.bfloat16)  65.2 us
    add x1, other arithmetic, long_mix(): result = result + tap_table[tap_index][None, :] * window * keep  44 us
    ppermute x3, waiting for transfers between devices, passed_along(): lax.ppermute(value, axis, [(source, source + steps) for source in range(f...  30.8 us
    dot_general x1, matrix products, body(): totals = jnp.dot(columns, flat_rows, preferred_element_type=jnp.float32)  26.1 us
    gather x1, local copies, waits for them, and re-layouts, body(): embedded = jnp.take(embed_table, new_ids, axis=0)  14.7 us
  transfers between devices with their start and end apart: 6, of which 4 were waited for; matrix products, arithmetic and copies ran while one was open for 49% of the time, Pallas kernels for 0%

commit v1 on v0

v1 whole, which is shorter than its diff:
```python
import functools

import jax
import jax.numpy as jnp
from jax import lax
from jax.experimental import pallas as pl
from jax.experimental.pallas import tpu as pltpu
from jax.sharding import PartitionSpec as P

ROWS = 768
HALO = 144
EXT = HALO + ROWS
TAPS = 128
CB = 256
LANES = 128
R = 32
GROUP = 4
MAX_PAIRS = ROWS // R + 32


def passed_along(value, axis, steps):
    count = lax.axis_size(axis)
    first, last = (max(0, -steps), min(count, count - steps))
    return lax.ppermute(value, axis, [(source, source + steps) for source in range(first, last)])


def conv_kernel(
    begin_ref,
    end_ref,
    ids_ref,
    age_ref,
    tab_ref,
    short_ref,
    filt_ref,
    decay_ref,
    out_ref,
    onehot,
    mask1,
    mask2,
    src,
    prod,
    window,
    taps,
    longs,
    pair_row,
    pair_begin,
    pair_end,
    pair_count,
):
    windows = begin_ref.shape[0]

    @pl.when(pl.program_id(0) == 0)
    def _():
        vocab = onehot.shape[1]
        ids = jnp.broadcast_to(ids_ref[...], (EXT, vocab))
        onehot[...] = jnp.where(ids == lax.broadcasted_iota(jnp.int32, (EXT, vocab), 1), 1.0, 0.0).astype(jnp.bfloat16)
        age = jnp.broadcast_to(age_ref[...], (EXT, LANES))
        mask1[...] = (age >= 1).astype(jnp.float32)
        mask2[...] = (age >= 2).astype(jnp.float32)
        src[:, 0:8, :] = jnp.zeros((3, 8, CB), jnp.float32)

        def per_window(w, count):
            low = jnp.maximum(begin_ref[w], HALO)
            high = jnp.minimum(end_ref[w], EXT)
            first = (low - HALO) // R
            last = jnp.where(high > low, (high - 1 - HALO) // R + 1, first)

            def per_piece(piece, k):
                pair_row[k] = HALO + piece * R
                pair_begin[k] = begin_ref[w]
                pair_end[k] = end_ref[w]
                return k + 1

            return lax.fori_loop(first, last, per_piece, count)

        pair_count[0] = lax.fori_loop(0, windows, per_window, 0)

    for g in range(3):
        table = tab_ref[:, g].reshape(CB, tab_ref.shape[3])
        src[g, 8:, :] = lax.dot_general(
            onehot[...], table, (((1,), (1,)), ((), ())), preferred_element_type=jnp.float32
        )
    tap_index = lax.broadcasted_iota(jnp.int32, (TAPS, CB), 0).astype(jnp.float32)
    taps[...] = filt_ref[...] * jnp.exp(-decay_ref[...] * tap_index)

    def mixed(g, low, count, lanes):
        return (
            short_ref[0, g : g + 1, lanes] * src[g, pl.ds(8 + low, count), lanes]
            + short_ref[1, g : g + 1, lanes] * (src[g, pl.ds(7 + low, count), lanes] * mask1[pl.ds(low, count), :])
            + short_ref[2, g : g + 1, lanes] * (src[g, pl.ds(6 + low, count), lanes] * mask2[pl.ds(low, count), :])
        )

    tiles = [slice(at, at + LANES) for at in range(0, CB, LANES)]
    for lanes in tiles:
        for low in range(0, EXT, 48):
            product = mixed(1, low, 48, lanes) * mixed(2, low, 48, lanes)
            prod[pl.ds(low, 48), lanes] = product.astype(jnp.bfloat16).astype(jnp.float32)

    def per_pair(k, carry):
        row = pl.multiple_of(pair_row[k], 16)
        begin = pair_begin[k]
        end = pair_end[k]
        at = row - TAPS + lax.broadcasted_iota(jnp.int32, (TAPS + R, LANES), 0)
        inside = (at >= begin) & (at < end)
        mine = inside[TAPS:]
        for lanes in tiles:
            window[...] = jnp.where(inside, prod[pl.ds(row - TAPS, TAPS + R), lanes], 0.0)
            sums = [jnp.zeros((8, LANES), jnp.float32) for _ in range(R // 8)]
            for phase in range(8):
                for block in range(0, TAPS // 8, GROUP):
                    held = [
                        jnp.broadcast_to(taps[pl.ds(phase + 8 * (block + m), 1), lanes], (8, LANES))
                        for m in range(GROUP)
                    ]
                    views = {
                        q: window[pl.ds(TAPS + 8 * q - phase, 8), :]
                        for q in range(-(block + GROUP - 1), R // 8 - block)
                    }
                    for i in range(R // 8):
                        for m in range(GROUP):
                            sums[i] = sums[i] + held[m] * views[i - block - m]
            result = jnp.concatenate(sums, axis=0)
            where = pl.ds(pl.multiple_of(row - HALO, 16), R)
            longs[where, lanes] = jnp.where(mine, result, longs[where, lanes])
        return carry

    lax.fori_loop(0, pair_count[0], per_pair, 0)
    for lanes in tiles:
        for low in range(0, ROWS, 48):
            gated = mixed(0, HALO + low, 48, lanes) * longs[pl.ds(low, 48), lanes]
            out_ref[pl.ds(low, 48), lanes] = gated.astype(jnp.bfloat16)


def gated_rows(begin, end, ids, age, table, short_filter, mr_filter, mr_decay, first, count):
    vocab = table.shape[3]
    steps = count // CB
    offset = first // CB
    smem = pl.BlockSpec(memory_space=pltpu.SMEM)
    return pl.pallas_call(
        conv_kernel,
        grid=(steps,),
        out_shape=jax.ShapeDtypeStruct((ROWS, count), jnp.bfloat16),
        in_specs=[
            smem,
            smem,
            pl.BlockSpec((EXT, 1), lambda i: (0, 0)),
            pl.BlockSpec((EXT, 1), lambda i: (0, 0)),
            pl.BlockSpec((CB // 32, 3, 32, vocab), lambda i: (i + offset, 0, 0, 0)),
            pl.BlockSpec((3, 3, CB), lambda i: (0, 0, i + offset)),
            pl.BlockSpec((TAPS, CB), lambda i: (0, i + offset)),
            pl.BlockSpec((1, CB), lambda i: (0, i + offset)),
        ],
        out_specs=pl.BlockSpec((ROWS, CB), lambda i: (0, i)),
        scratch_shapes=[
            pltpu.VMEM((EXT, vocab), jnp.bfloat16),
            pltpu.VMEM((EXT, LANES), jnp.float32),
            pltpu.VMEM((EXT, LANES), jnp.float32),
            pltpu.VMEM((3, EXT + 8, CB), jnp.float32),
            pltpu.VMEM((EXT, CB), jnp.float32),
            pltpu.VMEM((TAPS + R, LANES), jnp.float32),
            pltpu.VMEM((TAPS, CB), jnp.float32),
            pltpu.VMEM((ROWS, CB), jnp.float32),
            pltpu.SMEM((MAX_PAIRS,), jnp.int32),
            pltpu.SMEM((MAX_PAIRS,), jnp.int32),
            pltpu.SMEM((MAX_PAIRS,), jnp.int32),
            pltpu.SMEM((1,), jnp.int32),
        ],
        compiler_params=pltpu.CompilerParams(vmem_limit_bytes=40 * 2**20),
        cost_estimate=pl.CostEstimate(
            flops=2 * EXT * vocab * 3 * count + 100 * 2 * ROWS * count * TAPS,
            bytes_accessed=6 * vocab * count + 2 * ROWS * count,
            transcendentals=0,
        ),
    )(begin, end, ids, age, table, short_filter, mr_filter, mr_decay)


def body(
    token_ids,
    subst_pos,
    subst_base,
    window_lengths,
    embed_table,
    norm_gain,
    in_weight,
    short_filter,
    mr_filter,
    mr_decay,
    out_weight,
):
    row_count = token_ids.shape[0]
    channels = in_weight.shape[2]
    depth = in_weight.shape[0]
    vocab, width = embed_table.shape
    parts = lax.axis_size("context")
    copies = lax.axis_size("dp")
    each = channels // (parts * copies)

    shares = in_weight.reshape(depth, 3, parts, copies, each)
    shares = lax.dynamic_index_in_dim(shares, lax.axis_index("dp"), 3, keepdims=False)
    shares = shares.transpose(2, 1, 3, 0).reshape(parts, 3 * each, depth)
    shares = lax.all_to_all(shares, "context", 0, 0, tiled=True)
    x_wide = embed_table.astype(jnp.float32)
    scale = lax.rsqrt(jnp.mean(x_wide * x_wide, axis=1, keepdims=True) + 1e-06)
    normed = (x_wide * scale * norm_gain[None, :]).astype(jnp.bfloat16)
    own_weight = shares.transpose(1, 0, 2).reshape(3 * each, width)
    table = lax.dot_general(own_weight, normed, (((1,), (1,)), ((), ())), preferred_element_type=jnp.float32)
    table = lax.all_gather(table.astype(jnp.bfloat16), ("context", "dp"), axis=0, tiled=True)
    table = table.reshape(parts * copies, 3, each, vocab)

    matches = subst_pos[:, None] == jnp.arange(row_count, dtype=jnp.int32)[None, :]
    chosen = jnp.sum(jnp.where(matches, subst_base[:, None], 0), axis=0)
    touched = jnp.any(matches, axis=0)
    new_ids = jnp.where(touched, chosen, token_ids)
    before = passed_along(new_ids[row_count - HALO :], "context", 1)
    ids = jnp.concatenate([before, new_ids])

    first_row = lax.axis_index("context") * row_count - HALO
    ends = jnp.cumsum(window_lengths)
    starts = ends - window_lengths
    positions = first_row + jnp.arange(EXT, dtype=jnp.int32)
    begins = jnp.max(jnp.where(starts[None, :] <= positions[:, None], starts[None, :], -1), axis=1)
    age = jnp.where(begins >= 0, positions - begins, -1)

    def part(first, count):
        return gated_rows(
            starts - first_row,
            ends - first_row,
            ids[:, None],
            age[:, None],
            table,
            short_filter,
            mr_filter,
            mr_decay[None, :],
            first,
            count,
        )

    weight_in, table = lax.optimization_barrier((out_weight, table))
    weight_rows = lax.all_gather(weight_in, "context", axis=0, tiled=True)
    tensors = lax.axis_size("tensor")
    weight_rows = weight_rows.reshape(tensors, channels, out_weight.shape[1])
    own_columns = lax.dynamic_slice_in_dim(
        embed_table, lax.axis_index("tensor") * out_weight.shape[1], out_weight.shape[1], 1
    )
    picked = (new_ids[:, None] == jnp.arange(vocab, dtype=jnp.int32)[None, :]).astype(jnp.bfloat16)
    total = jnp.dot(picked, own_columns, preferred_element_type=jnp.float32)
    for first in range(0, channels, CB):
        features = lax.all_gather(part(first, CB), "tensor", axis=1, tiled=True)
        rows = weight_rows[:, first : first + CB].reshape(tensors * CB, -1)
        total = total + jnp.dot(features, rows, preferred_element_type=jnp.float32)
    return total.astype(jnp.bfloat16)


def solution(mesh):
    in_specs = (
        P(("dp", "context")),
        P(("dp", "context")),
        P(("dp", "context")),
        P("dp"),
        P(),
        P(),
        P("context", None, "tensor"),
        P(None, None, "tensor"),
        P(None, "tensor"),
        P("tensor"),
        P("context", "tensor"),
    )
    out_specs = P(("dp", "context"), "tensor")
    return jax.shard_map(body, mesh=mesh, in_specs=in_specs, out_specs=out_specs, check_vma=False)
```

time: 551 us -> 297 us (0.54); the launches traced: 541 us -> 296 us
  other arithmetic: 208 us -> 3.73 us
  waiting for transfers between devices: 236 us -> 171 us
  Pallas kernels: 0 us -> 50.8 us
  local copies, waits for them, and re-layouts: 35.4 us -> 17.7 us
  matrix products: 38.4 us -> 27.3 us
    concatenate x14 -> x1, other arithmetic: 80.7 us -> 0.07 us  [body(): ids = jnp.concatenate([before, new_ids])]
    convert_element_type x5 -> x0, other arithmetic: 67.3 us -> none  [the longest x1 65.2 us: body(): gated_out = (query_out * long_out).astype(jnp.bfloat16)]
    pallas_call x0 -> x4, Pallas kernels: none -> 50.8 us  [gated_rows(): pl.pallas_call(conv_kernel, grid=(steps,), out_shape=jax.ShapeDtypeStruct...]
    add x3 -> x1, other arithmetic: 48.3 us -> 0.01 us  [body(): positions = first_row + jnp.arange(EXT, dtype=jnp.int32)]
    all_gather x3 -> x6, waiting for transfers between devices: 204 us -> 160 us  [the longest x4 109 us: body(): features = lax.all_gather(part(first, CB), 'tensor', axis=1, tiled=True)]
    ppermute x3 -> x1, waiting for transfers between devices: 30.8 us -> 0.57 us  [passed_along(): lax.ppermute(value, axis, [(source, source + steps) for source in range(f...]
    gather x1 -> x0, local copies, waits for them, and re-layouts: 14.7 us -> none  [body(): embedded = jnp.take(embed_table, new_ids, axis=0)]
    all_to_all x0 -> x1, waiting for transfers between devices: none -> 11.2 us  [body(): shares = lax.all_to_all(shares, 'context', 0, 0, tiled=True)]
  transfers between devices with their start and end apart: 6 -> 8, of which waited for: 4 -> 8; matrix products, arithmetic and copies ran while one was open for 49% -> 9% of each run, Pallas kernels for 0% -> 17%
where the time goes in v1:
time: 297 us; the launch traced here: 296 us
  waiting for transfers between devices  171 us (58%)
  Pallas kernels  50.8 us (17%)
  matrix products  27.3 us (9%)
  local copies, waits for them, and re-layouts  17.7 us (6%)
  between operations  13.7 us (5%)
  starting transfers between devices  11.5 us (4%)
  other arithmetic  3.73 us (1%)
    all_gather x4, waiting for transfers between devices, body(): features = lax.all_gather(part(first, CB), 'tensor', axis=1, tiled=True)  109 us
    pallas_call x4, Pallas kernels, gated_rows(): pl.pallas_call(conv_kernel, grid=(steps,), out_shape=jax.ShapeDtypeStruct...  50.8 us
    all_gather x1, waiting for transfers between devices, body(): lax.all_gather(table.astype(jnp.bfloat16), ('context', 'dp'), axis=0, til...  43.2 us
    dot_general x4, matrix products, body(): total = total + jnp.dot(features, rows, preferred_element_type=jnp.float32)  18.9 us
    all_to_all x1, waiting for transfers between devices, body(): shares = lax.all_to_all(shares, 'context', 0, 0, tiled=True)  11.2 us
    unnamed x29, local copies, waits for them, and re-layouts  9.95 us
    all_to_all x1, starting transfers between devices, body(): shares = lax.all_to_all(shares, 'context', 0, 0, tiled=True)  7.96 us
    all_gather x1, waiting for transfers between devices, body(): weight_rows = lax.all_gather(weight_in, 'context', axis=0, tiled=True)  7.78 us
  transfers between devices with their start and end apart: 8, of which 8 were waited for; matrix products, arithmetic and copies ran while one was open for 9% of the time, Pallas kernels for 17%

profile of v1, /device:TPU:0, one launch (start us, length us, event | category | flops | bytes accessed | tf_op | source)
XLA Modules:
  0.0 296.1 jit_solution(10861652378019966811)
XLA Ops:
  6.5 1.7 copy.26
  8.2 0.1 dynamic-slice_bitcast_fusion
  8.3 0.9 copy.27
  9.3 8.0 %all-to-all-start = ((bf16[16,96,256]{2,1,0:T(8,128)(2,1)}), bf16[16,96,256]{2,1,0:T(8,128)(2,1)S(1)}, u32[]{:S(2)}, u32[]{:S(2)}) async-start(bf16[16,96,256]{2,1,0:T(8,128)(2,1)} %bitcast.6), calls=%async_computation | async-start | bytes 1572864 | tf_op jit(solution)/shard_map/all_to_all | solution.py:201
  17.2 0.0 all-gather.7.cloned.1.call-start
  17.3 3.1 %fusion = f32[512]{0:T(512)S(1)} fusion(bf16[512,4096]{1,0:T(8,128)(2,1)} %param.15), kind=kLoop, calls=%fused_computation.2 | loop fusion | flops 6290944 | bytes 4196352 | tf_op jit(solution)/shard_map/reduce_sum | solution.py:203
  20.4 11.2 %all-to-all-done = bf16[16,96,256]{2,1,0:T(8,128)(2,1)S(1)} async-done(((bf16[16,96,256]{2,1,0:T(8,128)(2,1)}), bf16[16,96,256]{2,1,0:T(8,128)(2,1)S(1)}, u32[]{:S(2)}, u32[]{:S(2)}) %all-to-all-start) | async-done | bytes 786464 | tf_op jit(solution)/shard_map/all_to_all | solution.py:201
  31.6 0.1 copy.33
  31.7 4.4 %fusion.7 = bf16[96,512]{1,0:T(8,128)(2,1)} fusion(bf16[96,4096]{1,0:T(8,128)(2,1)S(1)} %bitcast.43, bf16[512,4096]{1,0:T(8,128)(2,1)} %param.15, f32[4096]{0:T(1024)S(1)} %copy-done.13, f32[512]{0:T(512)S(1)} %add_rsqrt_fusion), kind=kOutput, calls=%fused_computation.10 | convolution fusion | flops 411090944 | bytes 5097472 | tf_op jit(solution)/shard_map/dot_general | solution.py:206
  36.2 0.0 all-gather.7.cloned.1.call-update
  36.2 0.0 all-gather.11.cloned.1.call-start
  36.2 43.2 %all-gather.7.cloned.1.call-done = bf16[3072,512]{1,0:T(8,128)(2,1)} async-done(((bf16[96,512]{1,0:T(8,128)(2,1)}), bf16[3072,512]{1,0:T(8,128)(2,1)}) %all-gather.7.cloned.1.call-update) | async-done | bytes 3145744 | tf_op jit(solution)/shard_map/all_gather | solution.py:207
  79.5 0.0 all-gather.17.cloned.1.call-start
  79.5 0.1 fusion.12
  79.7 0.1 select_reduce_fusion
  79.8 0.1 slice.15
  79.8 3.1 %collective-permute-start = (s32[144]{0:T(256)S(1)}, s32[144]{0:T(256)S(1)}, u32[]{:S(2)}, u32[]{:S(2)}) collective-permute-start(s32[144]{0:T(256)S(1)} %slice.15), channel_id=1, source_target_pairs={{0,4},{4,8},{8,12},{12,16},{16,20},{20,24},{24,28},{28,32},{32,36}... | collective-permute-start | bytes 1736 | tf_op jit(solution)/shard_map/ppermute | solution.py:24
  82.9 0.1 copy.23
  83.0 0.1 reduce-window.9
  83.1 0.1 reduce
  83.2 0.1 select_reduce_fusion.1
  83.3 0.2 copy.24
  83.6 0.1 subtract_select_fusion.age_ref
  83.6 0.6 collective-permute-done
  84.2 0.1 pad_add_fusion
  84.3 0.2 copy.29.ids_ref
  84.5 1.9 copy-done
  86.4 12.7 %shard_map.112 = bf16[768,256]{1,0:T(8,128)(2,1)} custom-call(s32[32]{0:T(128)S(1)} %get-tuple-element.9.begin_ref, s32[32]{0:T(128)S(1)} %get-tuple-element.15.end_ref, s32[912,1]{1,0:T(8,128)S(1)} %copy.29.ids_ref, s32[912,1]{1,0:T(8,128)S(1)} %subtract_select_fusion.age_ref, bf16[32,3,32,512]{3,2,1,0:T(8,128)(2,1)S(1)} %bitcast.28, ...), custom_call_target="tpu_custom_call" | custom-call | flops 5750390784 | bytes 1179648 | tf_op jit(solution)/shard_map/pallas_call | solution.py:139
  99.1 0.0 all-gather.15.cloned.1.call-start
  99.2 1.9 copy-done.1
  101.1 12.7 %shard_map.111 = bf16[768,256]{1,0:T(8,128)(2,1)} custom-call(s32[32]{0:T(128)S(1)} %get-tuple-element.9.begin_ref, s32[32]{0:T(128)S(1)} %get-tuple-element.15.end_ref, s32[912,1]{1,0:T(8,128)S(1)} %copy.29.ids_ref, s32[912,1]{1,0:T(8,128)S(1)} %subtract_select_fusion.age_ref, bf16[32,3,32,512]{3,2,1,0:T(8,128)(2,1)S(1)} %bitcast.29, ...), custom_call_target="tpu_custom_call" | custom-call | flops 5750390784 | bytes 1179648 | tf_op jit(solution)/shard_map/pallas_call | solution.py:139
  113.8 0.0 all-gather.9.cloned.1.call-start
  113.9 2.4 copy-done.2
  116.3 12.7 %shard_map.109 = bf16[768,256]{1,0:T(8,128)(2,1)} custom-call(s32[32]{0:T(128)S(1)} %get-tuple-element.9.begin_ref, s32[32]{0:T(128)S(1)} %get-tuple-element.15.end_ref, s32[912,1]{1,0:T(8,128)S(1)} %copy.29.ids_ref, s32[912,1]{1,0:T(8,128)S(1)} %subtract_select_fusion.age_ref, bf16[32,3,32,512]{3,2,1,0:T(8,128)(2,1)S(1)} %bitcast.30, ...), custom_call_target="tpu_custom_call" | custom-call | flops 5750390784 | bytes 1179648 | tf_op jit(solution)/shard_map/pallas_call | solution.py:139
  129.0 0.2 all-gather.13.cloned.1.call-start
  129.3 2.0 copy-done.3
  131.3 12.7 %shard_map.110 = bf16[768,256]{1,0:T(8,128)(2,1)} custom-call(s32[32]{0:T(128)S(1)} %get-tuple-element.9.begin_ref, s32[32]{0:T(128)S(1)} %get-tuple-element.15.end_ref, s32[912,1]{1,0:T(8,128)S(1)} %copy.29.ids_ref, s32[912,1]{1,0:T(8,128)S(1)} %subtract_select_fusion.age_ref, bf16[32,3,32,512]{3,2,1,0:T(8,128)(2,1)S(1)} %bitcast.31, ...), custom_call_target="tpu_custom_call" | custom-call | flops 5750390784 | bytes 1179648 | tf_op jit(solution)/shard_map/pallas_call | solution.py:139
  144.0 7.8 %all-gather.11.cloned.1.call-done = bf16[4096,1024]{1,0:T(8,128)(2,1)} async-done(((bf16[256,1024]{1,0:T(8,128)(2,1)}), bf16[4096,1024]{1,0:T(8,128)(2,1)}) %all-gather.11.cloned.1.call-update) | async-done | bytes 8388624 | tf_op jit(solution)/shard_map/all_gather | solution.py:239
  151.8 6.1 %fusion.14 = (bf16[4,256,1024]{2,1,0:T(8,128)(2,1)}, bf16[4,256,1024]{2,1,0:T(8,128)(2,1)}, bf16[4,256,1024]{2,1,0:T(8,128)(2,1)}, bf16[4,256,1024]{2,1,0:T(8,128)(2,1)}) fusion(bf16[4,1024,1024]{2,1,0:T(8,128)(2,1)} %bitcast.36), kind=kLoop, calls=%fused_computation.25 | loop fusion | bytes 16777216 | tf_op jit(solution)/shard_map/slice | solution.py:249
  157.9 25.4 %all-gather.17.cloned.1.call-done = bf16[768,1024]{1,0:T(8,128)(2,1)} async-done(((bf16[768,256]{1,0:T(8,128)(2,1)}), bf16[768,1024]{1,0:T(8,128)(2,1)}) %all-gather.17.cloned.1.call-update) | async-done | bytes 1572880 | tf_op jit(solution)/shard_map/all_gather | solution.py:248
  183.2 3.9 %fusion.18 = f32[768,1024]{1,0:T(8,128)S(1)} fusion(bf16[768,1024]{1,0:T(8,128)(2,1)} %all-gather.17.cloned.1.call-done, bf16[1024,1024]{1,0:T(8,128)(2,1)} %bitcast.42), kind=kOutput, calls=%fused_computation.29 | convolution fusion | flops 1610612736 | bytes 6815744 | tf_op jit(solution)/shard_map/dot_general | solution.py:250
  187.1 28.8 %all-gather.15.cloned.1.call-done = bf16[768,1024]{1,0:T(8,128)(2,1)} async-done(((bf16[768,256]{1,0:T(8,128)(2,1)}), bf16[768,1024]{1,0:T(8,128)(2,1)}) %all-gather.15.cloned.1.call-update) | async-done | bytes 1572880 | tf_op jit(solution)/shard_map/all_gather | solution.py:248
  215.9 5.5 %fusion.17 = f32[768,1024]{1,0:T(8,128)} fusion(bf16[768,1024]{1,0:T(8,128)(2,1)} %all-gather.15.cloned.1.call-done, bf16[1024,1024]{1,0:T(8,128)(2,1)} %bitcast.41), kind=kOutput, calls=%fused_computation.28 | convolution fusion | flops 1610612736 | bytes 6815744 | tf_op jit(solution)/shard_map/dot_general | solution.py:250
  221.4 27.2 %all-gather.9.cloned.1.call-done = bf16[768,1024]{1,0:T(8,128)(2,1)} async-done(((bf16[768,256]{1,0:T(8,128)(2,1)}), bf16[768,1024]{1,0:T(8,128)(2,1)}) %all-gather.9.cloned.1.call-update) | async-done | bytes 1572880 | tf_op jit(solution)/shard_map/all_gather | solution.py:248
  248.6 5.6 %fusion.15 = f32[768,1024]{1,0:T(8,128)} fusion(bf16[768,1024]{1,0:T(8,128)(2,1)} %all-gather.9.cloned.1.call-done, bf16[1024,1024]{1,0:T(8,128)(2,1)} %bitcast.40), kind=kOutput, calls=%fused_computation.26 | convolution fusion | flops 1610612736 | bytes 6815744 | tf_op jit(solution)/shard_map/dot_general | solution.py:250
  254.2 27.1 %all-gather.13.cloned.1.call-done = bf16[768,1024]{1,0:T(8,128)(2,1)} async-done(((bf16[768,256]{1,0:T(8,128)(2,1)}), bf16[768,1024]{1,0:T(8,128)(2,1)}) %all-gather.13.cloned.1.call-update) | async-done | bytes 1572880 | tf_op jit(solution)/shard_map/all_gather | solution.py:248
  281.3 4.0 %fusion.16 = f32[768,1024]{1,0:T(8,128)S(1)} fusion(bf16[768,1024]{1,0:T(8,128)(2,1)} %all-gather.13.cloned.1.call-done, bf16[1024,1024]{1,0:T(8,128)(2,1)} %bitcast.39), kind=kOutput, calls=%fused_computation.27 | convolution fusion | flops 1610612736 | bytes 6815744 | tf_op jit(solution)/shard_map/dot_general | solution.py:250
  285.4 3.9 %add_convert_fusion = bf16[768,1024]{1,0:T(8,128)(2,1)} fusion(f32[768,1024]{1,0:T(8,128)S(1)} %fusion.18, f32[768,1024]{1,0:T(8,128)S(1)} %copy-done.7, f32[768,1024]{1,0:T(8,128)S(1)} %fusion.16, f32[768,1024]{1,0:T(8,128)S(1)} %copy-done.8, bf16[512,4096]{1,0:T(8,128)(2,1)} %param.15, s32[]{:T(128)S(6)} %select_n.32, s32[768]{0:T(1024)S(1)} %select_n.31), kind=kOutput, calls=%fused_computation.8 | convolution fusion | flops 809631744 | bytes 15207428 | tf_op jit(solution)/shard_map/dot_general | solution.py:246
  (33 shorter events, 0.2 us)
Async XLA Ops:
  9.3 22.3 %all-to-all-start = ((bf16[16,96,256]{2,1,0:T(8,128)(2,1)}), bf16[16,96,256]{2,1,0:T(8,128)(2,1)S(1)}, u32[]{:S(2)}, u32[]{:S(2)}) async-start(bf16[16,96,256]{2,1,0:T(8,128)(2,1)} %bitcast.6), calls=%async_computation | async-start | bytes 1572864 | tf_op jit(solution)/shard_map/all_to_all | solution.py:201
  17.2 14.4 %copy-start.13 = (f32[4096]{0:T(1024)S(1)}, f32[4096]{0:T(1024)}, u32[]{:S(2)}) copy-start(f32[4096]{0:T(1024)} %param.16) | copy-start | bytes 49156
  17.2 62.2 %all-gather.7.cloned.1.call-start = ((), (), s32[]{:S(2)}) async-start(), calls=%async_computation.1 | async-start | bytes 3244032 | tf_op jit(solution)/shard_map/all_gather | solution.py:207
  31.7 47.9 %copy-start.11 = (s32[48]{0:T(128)S(1)}, s32[48]{0:T(128)}, u32[]{:S(2)}) copy-start(s32[48]{0:T(128)} %param.12) | copy-start | bytes 580
  31.7 48.0 %copy-start.12 = (s32[48]{0:T(128)S(1)}, s32[48]{0:T(128)}, u32[]{:S(2)}) copy-start(s32[48]{0:T(128)} %param.13) | copy-start | bytes 580
  31.7 48.1 %copy-start.9 = (s32[768]{0:T(1024)S(1)}, s32[768]{0:T(1024)}, u32[]{:S(2)}) copy-start(s32[768]{0:T(1024)} %param.11) | copy-start | bytes 9220
  31.7 51.2 %copy-start.10 = (s32[32]{0:T(128)S(1)}, s32[32]{0:T(128)}, u32[]{:S(2)}) copy-start(s32[32]{0:T(128)} %param.14) | copy-start | bytes 388
  36.2 48.4 %copy-start.4 = (f32[128,1024]{1,0:T(8,128)S(1)}, f32[128,1024]{1,0:T(8,128)}, u32[]{:S(2)}) copy-start(f32[128,1024]{1,0:T(8,128)} %filt_ref.7) | copy-start | bytes 1572868
  36.2 48.4 %copy-start.5 = (f32[3,3,1024]{2,1,0:T(4,128)S(1)}, f32[3,3,1024]{2,1,0:T(4,128)}, u32[]{:S(2)}) copy-start(f32[3,3,1024]{2,1,0:T(4,128)} %short_ref.7) | copy-start | bytes 110596
  36.2 48.4 %copy-start.6 = (f32[1024]{0:T(1024)S(1)}, f32[1024]{0:T(1024)}, u32[]{:S(2)}) copy-start(f32[1024]{0:T(1024)} %param.20) | copy-start | bytes 12292
  36.2 115.6 %all-gather.11.cloned.1.call-start = ((), (), s32[]{:S(2)}) async-start(), calls=%async_computation.3 | async-start | bytes 8912896 | tf_op jit(solution)/shard_map/all_gather | solution.py:239
  79.5 103.8 %all-gather.17.cloned.1.call-start = ((), (), s32[]{:S(2)}) async-start(), calls=%async_computation.6 | async-start | bytes 1966080 | tf_op jit(solution)/shard_map/all_gather | solution.py:248
  79.8 4.4 %collective-permute-start = (s32[144]{0:T(256)S(1)}, s32[144]{0:T(256)S(1)}, u32[]{:S(2)}, u32[]{:S(2)}) collective-permute-start(s32[144]{0:T(256)S(1)} %slice.15), channel_id=1, source_target_pairs={{0,4},{4,8},{8,12},{12,16},{16,20},{20,24},{24,28},{28,32},{32,36}... | collective-permute-start | bytes 1736 | tf_op jit(solution)/shard_map/ppermute | solution.py:24
  84.5 1.9 copy-start
  99.1 116.8 %all-gather.15.cloned.1.call-start = ((), (), s32[]{:S(2)}) async-start(), calls=%async_computation.5 | async-start | bytes 1966080 | tf_op jit(solution)/shard_map/all_gather | solution.py:248
  99.2 1.9 copy-start.1
  113.8 134.8 %all-gather.9.cloned.1.call-start = ((), (), s32[]{:S(2)}) async-start(), calls=%async_computation.2 | async-start | bytes 1966080 | tf_op jit(solution)/shard_map/all_gather | solution.py:248
  113.9 2.4 copy-start.2
  129.0 152.3 %all-gather.13.cloned.1.call-start = ((), (), s32[]{:S(2)}) async-start(), calls=%async_computation.4 | async-start | bytes 1966080 | tf_op jit(solution)/shard_map/all_gather | solution.py:248
  129.3 2.0 copy-start.3
  281.3 4.0 %copy-start.7 = (f32[768,1024]{1,0:T(8,128)S(1)}, f32[768,1024]{1,0:T(8,128)}, u32[]{:S(2)}) copy-start(f32[768,1024]{1,0:T(8,128)} %fusion.17) | copy-start | bytes 9437188
  281.3 4.0 %copy-start.8 = (f32[768,1024]{1,0:T(8,128)S(1)}, f32[768,1024]{1,0:T(8,128)}, u32[]{:S(2)}) copy-start(f32[768,1024]{1,0:T(8,128)} %fusion.15) | copy-start | bytes 9437188
Sparse Core Ops, SparseCore 0:
  36.3 43.1 all-gather.6
  81.6 70.1 all-gather.10
  153.4 29.7 all-gather.16
  184.8 31.1 all-gather.14
  217.4 31.1 all-gather.8
  250.1 31.1 all-gather.12

commit v2 on v0

v2 whole, which is shorter than its diff:
```python
import jax
import jax.numpy as jnp
from jax import lax
from jax.experimental import pallas as pl
from jax.experimental.pallas import tpu as pltpu
from jax.sharding import PartitionSpec as P

ROWS = 768
HALO = 144
EXT = HALO + ROWS
TAPS = 128
LANES = 128
R = 32
PIECES = ROWS // R
GROUP = 4
DEPTH = 256
SIDE = 4
PEERS = SIDE * SIDE
CHUNKS = 8
SHARE = 3 * LANES * CHUNKS // (2 * PEERS)
HALF = ROWS // 2
MESH = pl.DeviceIdType.MESH


def moved(c, k, sign):
    x = lax.rem(c // SIDE + SIDE + sign * (k // SIDE), SIDE)
    z = lax.rem(lax.rem(c, SIDE) + SIDE + sign * (k % SIDE), SIDE)
    return x * SIDE + z


def greet(axis_targets):
    barrier = pltpu.get_barrier_semaphore()
    for target in axis_targets:
        pl.semaphore_signal(barrier, inc=1, device_id=target, device_id_type=MESH)
    pl.semaphore_wait(barrier, len(axis_targets))


def send(source, target, sent, arrived, where):
    return pltpu.make_async_remote_copy(
        src_ref=source, dst_ref=target, send_sem=sent, recv_sem=arrived, device_id=where, device_id_type=MESH
    )


def table_kernel(
    shares,
    embed,
    gain,
    ids,
    table,
    before,
    got,
    normed,
    piece,
    sent_w,
    come_w,
    sent_t,
    come_t,
    sent_f,
    come_f,
    ids_sem,
    local_sem,
):
    d = lax.axis_index("dp")
    c = lax.axis_index("context")
    other = {"dp": 1 - d}
    following = lax.rem(c + 1, PEERS)
    previous = lax.rem(c + PEERS - 1, PEERS)
    greet(
        [{"context": moved(c, k, 1)} for k in range(1, PEERS)]
        + [other, {"context": following}, {"context": previous}]
    )
    weights = [
        send(shares.at[moved(c, k, 1)], got.at[c], sent_w.at[k], come_w.at[k], {"context": moved(c, k, 1)})
        for k in range(1, PEERS)
    ]
    for copy in weights:
        copy.start()
    ids_copy = send(ids, before, ids_sem.at[0], ids_sem.at[1], {"context": following})
    ids_copy.start()

    vocab, width = embed.shape
    step = 32

    def norm_rows(i, carry):
        rows = pl.ds(pl.multiple_of(i * step, step), step)
        wide = embed[rows, :].astype(jnp.float32)
        scale = lax.rsqrt(jnp.mean(wide * wide, axis=1, keepdims=True) + 1e-06)
        values = (wide * scale * gain[...]).astype(jnp.bfloat16)
        for s in range(PEERS):
            normed[s, rows, :] = values[:, s * DEPTH : (s + 1) * DEPTH]
        return carry

    lax.fori_loop(0, vocab // step, norm_rows, 0)

    def product(weight, s):
        return lax.dot_general(
            weight, normed[s], (((1,), (1,)), ((), ())), preferred_element_type=jnp.float32
        )

    total = product(shares[c], c)
    for k in range(1, PEERS):
        weights[k - 1].wait_recv()
        origin = moved(c, k, -1)
        total = total + product(got[origin], origin)
    piece[...] = total.astype(jnp.bfloat16)
    mine = table.at[2 * c + d]
    spread = [
        send(piece, mine, sent_t.at[k], come_t.at[k], {"context": moved(c, k, 1)}) for k in range(1, PEERS)
    ]
    forward = [send(piece, mine, sent_f.at[0], come_f.at[0], other)]
    forward[0].start()
    for copy in spread:
        copy.start()
    local = pltpu.make_async_copy(piece, mine, local_sem)
    local.start()
    for k in range(1, PEERS):
        spread[k - 1].wait_recv()
        slot = table.at[2 * moved(c, k, -1) + d]
        forward.append(send(slot, slot, sent_f.at[k], come_f.at[k], other))
        forward[k].start()
    for copy in forward:
        copy.wait_recv()
    for copy in weights + spread + forward:
        copy.wait_send()
    ids_copy.wait()
    local.wait()


def token_table(shares, embed, gain, ids):
    vmem = pl.BlockSpec(memory_space=pltpu.VMEM)
    anywhere = pl.BlockSpec(memory_space=pl.ANY)
    vocab, width = embed.shape
    semaphores = [pltpu.SemaphoreType.DMA((PEERS,))] * 6
    return pl.pallas_call(
        table_kernel,
        out_shape=(
            jax.ShapeDtypeStruct((2 * PEERS, SHARE, vocab), jnp.bfloat16),
            jax.ShapeDtypeStruct(ids.shape, jnp.int32),
        ),
        in_specs=[vmem, vmem, vmem, anywhere],
        out_specs=(anywhere, anywhere),
        scratch_shapes=[
            pltpu.VMEM((PEERS, SHARE, DEPTH), jnp.bfloat16),
            pltpu.VMEM((PEERS, vocab, DEPTH), jnp.bfloat16),
            pltpu.VMEM((SHARE, vocab), jnp.bfloat16),
            *semaphores,
            pltpu.SemaphoreType.DMA((2,)),
            pltpu.SemaphoreType.DMA,
        ],
        compiler_params=pltpu.CompilerParams(
            collective_id=0, has_side_effects=True, vmem_limit_bytes=40 * 2**20
        ),
        cost_estimate=pl.CostEstimate(flops=2 * SHARE * vocab * width, bytes_accessed=2**24, transcendentals=0),
    )(shares, embed, gain, ids)


def block_kernel(
    begin_ref,
    end_ref,
    ids_ref,
    age_ref,
    table,
    short_ref,
    filt_ref,
    decay_ref,
    columns,
    weight,
    out_ref,
    onehot,
    mask1,
    mask2,
    src,
    prod,
    window,
    taps,
    longs,
    gates,
    total,
    weights,
    sent_own,
    come_own,
    sent_pass,
    come_pass,
    sent_w,
    come_w,
    sent_f,
    come_f,
    local_sem,
):
    d = lax.axis_index("dp")
    c = lax.axis_index("context")
    t = lax.axis_index("tensor")
    right = lax.rem(t + 1, SIDE)
    left = lax.rem(t + SIDE - 1, SIDE)
    other = {"dp": 1 - d}
    greet(
        [{"tensor": right}, {"tensor": left}, other]
        + [{"context": moved(c, k, 1)} for k in range(1, PEERS)]
    )
    spread = [
        send(weight.at[d], weights.at[2 * c + d], sent_w.at[k], come_w.at[k], {"context": moved(c, k, 1)})
        for k in range(1, PEERS)
    ]
    for copy in spread:
        copy.start()
    local = [pltpu.make_async_copy(weight.at[h], weights.at[2 * c + h], local_sem.at[h]) for h in range(2)]
    for copy in local:
        copy.start()

    vocab = onehot.shape[1]
    ids = jnp.broadcast_to(ids_ref[...], (EXT, vocab))
    onehot[...] = jnp.where(ids == lax.broadcasted_iota(jnp.int32, (EXT, vocab), 1), 1.0, 0.0).astype(jnp.bfloat16)
    age = jnp.broadcast_to(age_ref[...], (EXT, LANES))
    mask1[...] = (age >= 1).astype(jnp.float32)
    mask2[...] = (age >= 2).astype(jnp.float32)
    src[0:8, :] = jnp.zeros((8, 3 * LANES), jnp.float32)

    def own_copies(i):
        return (
            send(gates.at[t, i], gates.at[t, i], sent_own.at[0, i], come_own.at[0, i], {"tensor": right}),
            send(gates.at[t, i], gates.at[t, i], sent_own.at[1, i], come_own.at[1, i], {"tensor": left}),
        )

    def pass_copies(i):
        low = (i, pl.ds(0, HALF))
        high = (i, pl.ds(HALF, HALF))
        return (
            send(gates.at[left, *low], gates.at[left, *low], sent_pass.at[0, i], come_pass.at[0, i], {"tensor": right}),
            send(gates.at[right, *high], gates.at[right, *high], sent_pass.at[1, i], come_pass.at[1, i], {"tensor": left}),
        )

    def hand_on(i):
        own, further = own_copies(i), pass_copies(i)
        for direction in range(2):
            own[direction].wait_recv()
            further[direction].start()

    def chunk(i, carry):
        pieces = table[pl.ds(i * 4, 4)].reshape(3 * LANES, vocab)
        src[8:, :] = lax.dot_general(
            onehot[...], pieces, (((1,), (1,)), ((), ())), preferred_element_type=jnp.float32
        )
        tap_index = lax.broadcasted_iota(jnp.int32, (TAPS, LANES), 0).astype(jnp.float32)
        taps[...] = filt_ref[i] * jnp.exp(-decay_ref[i] * tap_index)
        filters = short_ref[i]

        def mixed(g, low, count):
            lanes = slice(g * LANES, (g + 1) * LANES)
            return (
                filters[0, g : g + 1] * src[pl.ds(8 + low, count), lanes]
                + filters[1, g : g + 1] * (src[pl.ds(7 + low, count), lanes] * mask1[pl.ds(low, count), :])
                + filters[2, g : g + 1] * (src[pl.ds(6 + low, count), lanes] * mask2[pl.ds(low, count), :])
            )

        for low in range(0, EXT, 48):
            product = mixed(1, low, 48) * mixed(2, low, 48)
            prod[pl.ds(low, 48), :] = product.astype(jnp.bfloat16).astype(jnp.float32)

        def piece(n, carry):
            row = pl.multiple_of(HALO + n * R, 16)
            begin = begin_ref[n]
            end = end_ref[n]
            at = row - TAPS + lax.broadcasted_iota(jnp.int32, (TAPS + R, LANES), 0)
            inside = (at >= begin) & (at < end)
            values = prod[pl.ds(row - TAPS, TAPS + R), :]
            window[0] = jnp.where(inside, values, 0.0)
            window[1, TAPS - 8 :] = values[TAPS - 8 :]
            ages = jnp.broadcast_to(age_ref[pl.ds(row, R), :], (R, LANES))
            sums = [jnp.zeros((8, LANES), jnp.float32) for _ in range(R // 8)]
            late = [jnp.zeros((8, LANES), jnp.float32) for _ in range(R // 8)]
            for phase in range(8):
                for block in range(0, TAPS // 8, GROUP):
                    held = [
                        jnp.broadcast_to(taps[pl.ds(phase + 8 * (block + m), 1), :], (8, LANES))
                        for m in range(GROUP)
                    ]
                    views = {
                        q: window[0, pl.ds(TAPS + 8 * q - phase, 8), :]
                        for q in range(-(block + GROUP - 1), R // 8 - block)
                    }
                    for i in range(R // 8):
                        for m in range(GROUP):
                            sums[i] = sums[i] + held[m] * views[i - block - m]
                    if block < R // 8:
                        starts = {q: window[1, pl.ds(TAPS + 8 * q - phase, 8), :] for q in range(R // 8)}
                        for i in range(R // 8):
                            for m in range(GROUP):
                                q = i - block - m
                                if q < 0:
                                    continue
                                kept = ages[8 * i : 8 * i + 8] >= phase + 8 * (block + m)
                                late[i] = late[i] + held[m] * jnp.where(kept, starts[q], 0.0)
            result = jnp.where(
                at[TAPS:] < end, jnp.concatenate(sums, axis=0), jnp.concatenate(late, axis=0)
            )
            longs[pl.ds(pl.multiple_of(n * R, R), R), :] = result
            return carry

        lax.fori_loop(0, PIECES, piece, 0)
        for low in range(0, ROWS, 48):
            gated = mixed(0, HALO + low, 48) * longs[pl.ds(low, 48), :]
            gates[t, i, pl.ds(low, 48), :] = gated.astype(jnp.bfloat16)
        for copy in own_copies(i):
            copy.start()

        @pl.when(i > 0)
        def _():
            hand_on(i - 1)

        return carry

    lax.fori_loop(0, CHUNKS, chunk, 0)
    hand_on(CHUNKS - 1)

    forward = []
    for k in range(1, PEERS):
        spread[k - 1].wait_recv()
        slot = weights.at[2 * moved(c, k, -1) + d]
        forward.append(send(slot, slot, sent_f.at[k], come_f.at[k], other))
        forward[k - 1].start()
    total[...] = jnp.dot(onehot[HALO:, :], columns[...], preferred_element_type=jnp.float32)
    for copy in local:
        copy.wait()
    for copy in forward:
        copy.wait_recv()

    def finish(i, carry):
        for copy in pass_copies(i):
            copy.wait_recv()
        features = jnp.concatenate([gates[s, i] for s in range(SIDE)], axis=1)
        rows = jnp.concatenate([weights[s * CHUNKS + i] for s in range(SIDE)], axis=0)
        total[...] += jnp.dot(features, rows, preferred_element_type=jnp.float32)
        return carry

    lax.fori_loop(0, CHUNKS, finish, 0)
    out_ref[...] = total[...].astype(jnp.bfloat16)

    def drain(i, carry):
        for copy in own_copies(i) + pass_copies(i):
            copy.wait_send()
        return carry

    lax.fori_loop(0, CHUNKS, drain, 0)
    for copy in spread + forward:
        copy.wait_send()


def block_rows(begin, end, ids, age, table, short_filter, mr_filter, mr_decay, columns, weight):
    vocab = table.shape[2]
    width = columns.shape[1]
    smem = pl.BlockSpec(memory_space=pltpu.SMEM)
    vmem = pl.BlockSpec(memory_space=pltpu.VMEM)
    return pl.pallas_call(
        block_kernel,
        out_shape=jax.ShapeDtypeStruct((ROWS, width), jnp.bfloat16),
        in_specs=[smem, smem] + [vmem] * 8,
        out_specs=vmem,
        scratch_shapes=[
            pltpu.VMEM((EXT, vocab), jnp.bfloat16),
            pltpu.VMEM((EXT, LANES), jnp.float32),
            pltpu.VMEM((EXT, LANES), jnp.float32),
            pltpu.VMEM((EXT + 8, 3 * LANES), jnp.float32),
            pltpu.VMEM((EXT, LANES), jnp.float32),
            pltpu.VMEM((2, TAPS + R, LANES), jnp.float32),
            pltpu.VMEM((TAPS, LANES), jnp.float32),
            pltpu.VMEM((ROWS, LANES), jnp.float32),
            pltpu.VMEM((SIDE, CHUNKS, ROWS, LANES), jnp.bfloat16),
            pltpu.VMEM((ROWS, width), jnp.float32),
            pltpu.VMEM((2 * PEERS, DEPTH // 2, width), jnp.bfloat16),
            pltpu.SemaphoreType.DMA((2, CHUNKS)),
            pltpu.SemaphoreType.DMA((2, CHUNKS)),
            pltpu.SemaphoreType.DMA((2, CHUNKS)),
            pltpu.SemaphoreType.DMA((2, CHUNKS)),
            pltpu.SemaphoreType.DMA((PEERS,)),
            pltpu.SemaphoreType.DMA((PEERS,)),
            pltpu.SemaphoreType.DMA((PEERS,)),
            pltpu.SemaphoreType.DMA((PEERS,)),
            pltpu.SemaphoreType.DMA((2,)),
        ],
        compiler_params=pltpu.CompilerParams(
            collective_id=1, has_side_effects=True, vmem_limit_bytes=56 * 2**20
        ),
        cost_estimate=pl.CostEstimate(flops=2 * ROWS * width * 4096, bytes_accessed=2**24, transcendentals=0),
    )(begin, end, ids, age, table, short_filter, mr_filter, mr_decay, columns, weight)


def body(
    token_ids,
    subst_pos,
    subst_base,
    window_lengths,
    embed_table,
    norm_gain,
    in_weight,
    short_filter,
    mr_filter,
    mr_decay,
    out_weight,
):
    row_count = token_ids.shape[0]
    vocab = embed_table.shape[0]
    width = out_weight.shape[1]

    matches = subst_pos[:, None] == jnp.arange(row_count, dtype=jnp.int32)[None, :]
    chosen = jnp.sum(jnp.where(matches, subst_base[:, None], 0), axis=0)
    touched = jnp.any(matches, axis=0)
    new_ids = jnp.where(touched, chosen, token_ids)

    shares = in_weight.reshape(DEPTH, 3, CHUNKS, LANES).transpose(2, 1, 3, 0).reshape(PEERS, 2, SHARE, DEPTH)
    shares = lax.dynamic_index_in_dim(shares, lax.axis_index("dp"), 1, keepdims=False)
    table, before = token_table(shares, embed_table, norm_gain[None, :], new_ids.reshape(-1, LANES))
    ids = jnp.concatenate([before.reshape(-1)[row_count - HALO :], new_ids])

    first_row = lax.axis_index("context") * row_count - HALO
    ends = jnp.cumsum(window_lengths)
    starts = ends - window_lengths
    positions = first_row + jnp.arange(EXT, dtype=jnp.int32)
    begins = jnp.max(jnp.where(starts[None, :] <= positions[:, None], starts[None, :], -1), axis=1)
    age = jnp.where(begins >= 0, positions - begins, -1)
    heads = first_row + HALO + R * jnp.arange(PIECES, dtype=jnp.int32)
    head_begin = jnp.max(jnp.where(starts[None, :] <= heads[:, None], starts[None, :], -1), axis=1)
    head_end = jnp.min(jnp.where(ends[None, :] > heads[:, None], ends[None, :], 1 << 20), axis=1)

    columns = lax.dynamic_slice_in_dim(embed_table, lax.axis_index("tensor") * width, width, 1)
    return block_rows(
        head_begin - first_row,
        head_end - first_row,
        ids[:, None],
        age[:, None],
        table,
        short_filter.reshape(3, 3, CHUNKS, LANES).transpose(2, 0, 1, 3),
        mr_filter.reshape(TAPS, CHUNKS, LANES).transpose(1, 0, 2),
        mr_decay.reshape(CHUNKS, 1, LANES),
        columns,
        out_weight.reshape(2, DEPTH // 2, width),
    )


def solution(mesh):
    in_specs = (
        P(("dp", "context")),
        P(("dp", "context")),
        P(("dp", "context")),
        P("dp"),
        P(),
        P(),
        P("context", None, "tensor"),
        P(None, None, "tensor"),
        P(None, "tensor"),
        P("tensor"),
        P("context", "tensor"),
    )
    out_specs = P(("dp", "context"), "tensor")
    return jax.shard_map(body, mesh=mesh, in_specs=in_specs, out_specs=out_specs, check_vma=False)
```

time: 551 us -> 152 us (0.28)
  the two profiles are of different devices: /device:TPU:0 before, /device:TPU:13 now
where the time goes in v2:
time: 152 us; the launch traced here: 151 us
  Pallas kernels  132 us (87%)
  local copies, waits for them, and re-layouts  14.1 us (9%)
  other arithmetic  4.92 us (3%)
    pallas_call x1, Pallas kernels, block_rows(): pl.pallas_call(block_kernel, out_shape=jax.ShapeDtypeStruct((ROWS, width)...  91.8 us
    pallas_call x1, Pallas kernels, token_table(): pl.pallas_call(table_kernel, out_shape=(jax.ShapeDtypeStruct((2 * PEERS,...  40.4 us
    unnamed x13, local copies, waits for them, and re-layouts  7.2 us

profile of v2, /device:TPU:13, one launch (start us, length us, event | category | flops | bytes accessed | tf_op | source)
XLA Modules:
  0.0 151.3 jit_solution(14721969673567405448)
XLA Ops:
  0.0 0.0 copy-start.4
  0.0 0.8 fusion
  0.8 0.8 select_reduce_fusion
  1.6 0.7 select_n.41
  2.3 0.7 copy.29
  3.0 0.1 reduce-window.8
  3.1 0.1 reduce
  3.2 0.7 sub.26
  3.9 0.1 select_reduce_fusion.1
  4.0 0.2 select_reduce_fusion.2
  4.2 0.6 broadcast_subtract_fusion
  4.7 0.8 reshape.83
  5.6 0.6 copy.39
  6.2 0.2 copy.32
  6.4 0.9 subtract_select_fusion.age_ref
  7.3 0.0 copy-done.4
  7.3 0.2 copy.35
  7.5 0.0 copy-start.3
  7.5 1.0 copy.36
  8.5 2.3 %constant_dynamic-slice_fusion.columns = bf16[512,1024]{1,0:T(8,128)(2,1)} fusion(bf16[512,4096]{1,0:T(8,128)(2,1)} %embed.1, s32[]{:T(128)S(6)} %select_n.44), kind=kLoop, calls=%fused_computation.12 | loop fusion | bytes 2097156 | tf_op jit(solution)/shard_map/dynamic_slice | solution.py:424
  10.8 0.0 copy-done.3
  10.8 0.7 copy.30
  11.5 0.0 copy-start
  11.5 0.1 copy.31
  11.6 0.0 copy-start.1
  11.6 0.1 dynamic-slice_bitcast_fusion.shares
  11.7 2.0 %copy-done = bf16[512,4096]{1,0:T(8,128)(2,1)S(1)} copy-done((bf16[512,4096]{1,0:T(8,128)(2,1)S(1)}, bf16[512,4096]{1,0:T(8,128)(2,1)}, u32[]{:S(2)}) %copy-start) | copy-done | bytes 4194328
  13.7 0.0 copy-done.1
  13.7 40.4 %shard_map.109 = (bf16[32,96,512]{2,1,0:T(8,128)(2,1)S(1)}, s32[6,128]{1,0:T(8,128)S(1)}) custom-call(bf16[16,96,256]{2,1,0:T(8,128)(2,1)S(1)} %dynamic-slice_bitcast_fusion.shares, bf16[512,4096]{1,0:T(8,128)(2,1)S(1)} %copy-done, f32[1,4096]{1,0:T(1,128)S(1)} %bitcast.20, s32[6,128]{1,0:T(8,128)S(1)} %bitcast.19), custom_call_target="tpu_custom_call" | custom-call | flops 402653184 | bytes 16777216 | tf_op jit(solution)/shard_map/pallas_call | solution.py:134
  54.0 0.0 copy-start.2
  54.0 1.7 %copy-done.2 = bf16[32,96,512]{2,1,0:T(8,128)(2,1)} copy-done((bf16[32,96,512]{2,1,0:T(8,128)(2,1)}, bf16[32,96,512]{2,1,0:T(8,128)(2,1)S(1)}, u32[]{:S(2)}) %copy-start.2) | copy-done | bytes 3145752
  55.7 0.1 slice.3
  55.8 0.1 pad_add_fusion
  55.8 1.0 copy.37.ids_ref
  56.8 91.8 %shard_map.110 = bf16[768,1024]{1,0:T(8,128)(2,1)} custom-call(s32[24]{0:T(128)} %get-tuple-element.12.begin_ref, s32[24]{0:T(128)} %get-tuple-element.11.end_ref, s32[912,1]{1,0:T(8,128)} %copy.37.ids_ref, s32[912,1]{1,0:T(8,128)} %subtract_select_fusion.age_ref, bf16[32,96,512]{2,1,0:T(8,128)(2,1)} %copy-done.2, f32[8,3,3,128]{3,2,1,0:T(4,128)} %bitcast.26, ...), custom_call_target="tpu_custom_call" | custom-call | flops 6442450944 | bytes 16777216 | tf_op jit(solution)/shard_map/pallas_call | solution.py:353
  148.7 2.7 %copy.41 = bf16[768,1024]{1,0:T(8,128)(2,1)} copy(bf16[768,1024]{1,0:T(8,128)(2,1)} %shard_map.110) | data formatting | bytes 3145728
  (2 shorter events, 0.0 us)
Async XLA Ops:
  0.0 7.3 %copy-start.4 = (f32[128,1024]{1,0:T(8,128)S(1)}, f32[128,1024]{1,0:T(8,128)}, u32[]{:S(2)}) copy-start(f32[128,1024]{1,0:T(8,128)} %param.19) | copy-start | bytes 1572868
  7.5 3.3 %copy-start.3 = (bf16[256,3,1024]{2,0,1:T(8,128)(2,1)S(1)}, bf16[256,3,1024]{2,0,1:T(8,128)(2,1)}, u32[]{:S(2)}) copy-start(bf16[256,3,1024]{2,0,1:T(8,128)(2,1)} %param.17) | copy-start | bytes 4718596
  11.5 2.2 %copy-start = (bf16[512,4096]{1,0:T(8,128)(2,1)S(1)}, bf16[512,4096]{1,0:T(8,128)(2,1)}, u32[]{:S(2)}) copy-start(bf16[512,4096]{1,0:T(8,128)(2,1)} %embed.1) | copy-start | bytes 12582916
  11.6 2.1 %copy-start.1 = (f32[4096]{0:T(1024)S(1)}, f32[4096]{0:T(1024)}, u32[]{:S(2)}) copy-start(f32[4096]{0:T(1024)} %param.16) | copy-start | bytes 49156
  54.0 1.7 %copy-start.2 = (bf16[32,96,512]{2,1,0:T(8,128)(2,1)}, bf16[32,96,512]{2,1,0:T(8,128)(2,1)S(1)}, u32[]{:S(2)}) copy-start(bf16[32,96,512]{2,1,0:T(8,128)(2,1)S(1)} %get-tuple-element.8.table) | copy-start | bytes 9437188

commit v3 on v2

--- a/solution.py
+++ b/solution.py
@@ -39,6 +39,114 @@
     return pltpu.make_async_remote_copy(
         src_ref=source, dst_ref=target, send_sem=sent, recv_sem=arrived, device_id=where, device_id_type=MESH
     )
+
+
+class Ring:
+    def __init__(self, buffer, half, sent, come):
+        d = lax.axis_index("dp")
+        c = lax.axis_index("context")
+        self.x, self.z, self.d = c // SIDE, lax.rem(c, SIDE), d
+        self.buffer, self.sent, self.come = buffer, sent, come
+        self.low, self.high = pl.ds(0, half), pl.ds(half, half)
+
+    def context(self, j, m):
+        dx = (1 - self.d) * m + self.d * j
+        dz = (1 - self.d) * j + self.d * m
+        return lax.rem(self.x + dx, SIDE) * SIDE + lax.rem(self.z + dz, SIDE)
+
+    def copy(self, j, m, part, index, where):
+        at = 2 * self.context(j, m) + self.d
+        slot = self.buffer.at[at] if part is None else self.buffer.at[at, part]
+        return send(slot, slot, self.sent.at[index], self.come.at[index], where)
+
+    def along_a(self, side):
+        return {"context": self.context(3 if side else 1, 0)}
+
+    def along_b(self, side):
+        return {"context": self.context(0, 3 if side else 1)}
+
+    def first(self, side):
+        return self.copy(0, 0, None, side, self.along_a(side))
+
+    def second(self, side):
+        return self.copy(1 if side else 3, 0, self.high if side else self.low, 2 + side, self.along_a(side))
+
+    def third(self, j, side):
+        return self.copy(j, 0, None, 4 + 2 * j + side, self.along_b(side))
+
+    def fourth(self, j, side):
+        return self.copy(
+            j, 1 if side else 3, self.high if side else self.low, 12 + 2 * j + side, self.along_b(side)
+        )
+
+    def across(self, j, m):
+        return self.copy(j, m, None, 20 + 4 * j + m, {"dp": 1 - self.d})
+
+    def cross(self, *slots):
+        for j, m in slots:
+            self.across(j, m).start()
+
+    def crossed(self, *slots):
+        for j, m in slots:
+            self.across(j, m).wait_recv()
+
+    def hop1(self):
+        for side in range(2):
+            self.first(side).start()
+            self.third(0, side).start()
+
+    def hop2(self):
+        for side in range(2):
+            self.first(side).wait_recv()
+            self.second(side).start()
+            self.third(0, side).wait_recv()
+            self.fourth(0, side).start()
+        self.cross(*self.set2)
+        for j in (1, 3):
+            for side in range(2):
+                self.third(j, side).start()
+
+    def hop3(self):
+        for side in range(2):
+            self.second(side).wait_recv()
+        for side in range(2):
+            self.third(2, side).start()
+        for side in range(2):
+            self.fourth(0, side).wait_recv()
+        for j in (1, 3):
+            for side in range(2):
+                self.third(j, side).wait_recv()
+                self.fourth(j, side).start()
+        self.cross(*self.set3)
+
+    def hop4(self):
+        for side in range(2):
+            self.third(2, side).wait_recv()
+            self.fourth(2, side).start()
+        for j in (1, 3):
+            for side in range(2):
+                self.fourth(j, side).wait_recv()
+        self.cross(*self.set4)
+
+    def hop5(self):
+        for side in range(2):
+            self.fourth(2, side).wait_recv()
+        self.cross(*self.set5)
+
+    set2 = ((1, 0), (3, 0), (0, 1), (0, 3))
+    set3 = ((2, 0), (0, 2), (1, 1), (1, 3), (3, 1), (3, 3))
+    set4 = ((2, 1), (2, 3), (1, 2), (3, 2))
+    set5 = ((2, 2),)
+
+    def drain(self):
+        for side in range(2):
+            self.first(side).wait_send()
+            self.second(side).wait_send()
+            for j in range(SIDE):
+                self.third(j, side).wait_send()
+                self.fourth(j, side).wait_send()
+        for j, m in self.set2 + self.set3 + self.set4 + self.set5:
+            self.across(j, m).wait_send()
 
 
 def table_kernel(
@@ -172,6 +280,7 @@
     src,
     prod,
     window,
+    recent,
     taps,
     longs,
     gates,
@@ -183,8 +292,6 @@
     come_pass,
     sent_w,
     come_w,
-    sent_f,
-    come_f,
     local_sem,
 ):
     d = lax.axis_index("dp")
@@ -197,15 +304,10 @@
         [{"tensor": right}, {"tensor": left}, other]
         + [{"context": moved(c, k, 1)} for k in range(1, PEERS)]
     )
-    spread = [
-        send(weight.at[d], weights.at[2 * c + d], sent_w.at[k], come_w.at[k], {"context": moved(c, k, 1)})
-        for k in range(1, PEERS)
-    ]
-    for copy in spread:
-        copy.start()
     local = [pltpu.make_async_copy(weight.at[h], weights.at[2 * c + h], local_sem.at[h]) for h in range(2)]
     for copy in local:
         copy.start()
+    outs = Ring(weights, LANES // 2, sent_w, come_w)
 
     vocab = onehot.shape[1]
     ids = jnp.broadcast_to(ids_ref[...], (EXT, vocab))
@@ -214,6 +316,9 @@
     mask1[...] = (age >= 1).astype(jnp.float32)
     mask2[...] = (age >= 2).astype(jnp.float32)
     src[0:8, :] = jnp.zeros((8, 3 * LANES), jnp.float32)
+    for copy in local:
+        copy.wait()
+    outs.hop1()
 
     def own_copies(i):
         return (
@@ -236,6 +341,9 @@
             further[direction].start()
 
     def chunk(i, carry):
+        for at, hop in ((1, outs.hop2), (2, outs.hop3), (4, outs.hop4), (5, outs.hop5)):
+            pl.when(i == at)(hop)
+
         pieces = table[pl.ds(i * 4, 4)].reshape(3 * LANES, vocab)
         src[8:, :] = lax.dot_general(
             onehot[...], pieces, (((1,), (1,)), ((), ())), preferred_element_type=jnp.float32
@@ -260,14 +368,12 @@
             row = pl.multiple_of(HALO + n * R, 16)
             begin = begin_ref[n]
             end = end_ref[n]
-            at = row - TAPS + lax.broadcasted_iota(jnp.int32, (TAPS + R, LANES), 0)
-            inside = (at >= begin) & (at < end)
-            values = prod[pl.ds(row - TAPS, TAPS + R), :]
-            window[0] = jnp.where(inside, values, 0.0)
-            window[1, TAPS - 8 :] = values[TAPS - 8 :]
-            ages = jnp.broadcast_to(age_ref[pl.ds(row, R), :], (R, LANES))
+            before = row - TAPS + lax.broadcasted_iota(jnp.int32, (TAPS, LANES), 0)
+            window[...] = jnp.where(before >= begin, prod[pl.ds(row - TAPS, TAPS), :], 0.0)
+            recent[...] = prod[pl.ds(row - 8, R + 8), :]
+            age = jnp.broadcast_to(age_ref[pl.ds(row, R), :], (R, LANES))
             sums = [jnp.zeros((8, LANES), jnp.float32) for _ in range(R // 8)]
-            late = [jnp.zeros((8, LANES), jnp.float32) for _ in range(R // 8)]
+            near = [jnp.zeros((8, LANES), jnp.float32) for _ in range(R // 8)]
             for phase in range(8):
                 for block in range(0, TAPS // 8, GROUP):
                     held = [
@@ -275,24 +381,21 @@
                         for m in range(GROUP)
                     ]
                     views = {
-                        q: window[0, pl.ds(TAPS + 8 * q - phase, 8), :]
+                        q: window[pl.ds(TAPS + 8 * q - phase, 8), :]
+                        if q < 0
+                        else recent[pl.ds(8 + 8 * q - phase, 8), :]
                         for q in range(-(block + GROUP - 1), R // 8 - block)
                     }
                     for i in range(R // 8):
                         for m in range(GROUP):
-                            sums[i] = sums[i] + held[m] * views[i - block - m]
-                    if block < R // 8:
-                        starts = {q: window[1, pl.ds(TAPS + 8 * q - phase, 8), :] for q in range(R // 8)}
-                        for i in range(R // 8):
-                            for m in range(GROUP):
-                                q = i - block - m
-                                if q < 0:
-                                    continue
-                                kept = ages[8 * i : 8 * i + 8] >= phase + 8 * (block + m)
-                                late[i] = late[i] + held[m] * jnp.where(kept, starts[q], 0.0)
-            result = jnp.where(
-                at[TAPS:] < end, jnp.concatenate(sums, axis=0), jnp.concatenate(late, axis=0)
-            )
+                            q = i - block - m
+                            if q < 0:
+                                sums[i] = sums[i] + held[m] * views[q]
+                            else:
+                                kept = age[8 * i : 8 * i + 8] >= phase + 8 * (block + m)
+                                near[i] = near[i] + held[m] * jnp.where(kept, views[q], 0.0)
+            mine = row + lax.broadcasted_iota(jnp.int32, (R, LANES), 0) < end
+            result = jnp.where(mine, jnp.concatenate(sums, axis=0), 0.0) + jnp.concatenate(near, axis=0)
             longs[pl.ds(pl.multiple_of(n * R, R), R), :] = result
             return carry
 
@@ -312,17 +415,8 @@
     lax.fori_loop(0, CHUNKS, chunk, 0)
     hand_on(CHUNKS - 1)
 
-    forward = []
-    for k in range(1, PEERS):
-        spread[k - 1].wait_recv()
-        slot = weights.at[2 * moved(c, k, -1) + d]
-        forward.append(send(slot, slot, sent_f.at[k], come_f.at[k], other))
-        forward[k - 1].start()
     total[...] = jnp.dot(onehot[HALO:, :], columns[...], preferred_element_type=jnp.float32)
-    for copy in local:
-        copy.wait()
-    for copy in forward:
-        copy.wait_recv()
+    outs.crossed(*Ring.set2, *Ring.set3, *Ring.set4, *Ring.set5)
 
     def finish(i, carry):
         for copy in pass_copies(i):
@@ -341,8 +435,7 @@
         return carry
 
     lax.fori_loop(0, CHUNKS, drain, 0)
-    for copy in spread + forward:
-        copy.wait_send()
+    outs.drain()
 
 
 def block_rows(begin, end, ids, age, table, short_filter, mr_filter, mr_decay, columns, weight):
@@ -361,7 +454,8 @@
             pltpu.VMEM((EXT, LANES), jnp.float32),
             pltpu.VMEM((EXT + 8, 3 * LANES), jnp.float32),
             pltpu.VMEM((EXT, LANES), jnp.float32),
-            pltpu.VMEM((2, TAPS + R, LANES), jnp.float32),
+            pltpu.VMEM((TAPS, LANES), jnp.float32),
+            pltpu.VMEM((R + 8, LANES), jnp.float32),
             pltpu.VMEM((TAPS, LANES), jnp.float32),
             pltpu.VMEM((ROWS, LANES), jnp.float32),
             pltpu.VMEM((SIDE, CHUNKS, ROWS, LANES), jnp.bfloat16),
@@ -371,10 +465,8 @@
             pltpu.SemaphoreType.DMA((2, CHUNKS)),
             pltpu.SemaphoreType.DMA((2, CHUNKS)),
             pltpu.SemaphoreType.DMA((2, CHUNKS)),
-            pltpu.SemaphoreType.DMA((PEERS,)),
-            pltpu.SemaphoreType.DMA((PEERS,)),
-            pltpu.SemaphoreType.DMA((PEERS,)),
-            pltpu.SemaphoreType.DMA((PEERS,)),
+            pltpu.SemaphoreType.DMA((36,)),
+            pltpu.SemaphoreType.DMA((36,)),
             pltpu.SemaphoreType.DMA((2,)),
         ],
         compiler_params=pltpu.CompilerParams(

time: 152 us -> 144 us (0.947)
  the two profiles are of different devices: /device:TPU:13 before, /device:TPU:0 now
where the time goes in v3:
time: 144 us; the launch traced here: 143 us
  Pallas kernels  124 us (86%)
  local copies, waits for them, and re-layouts  14.1 us (10%)
  other arithmetic  4.92 us (3%)
    pallas_call x1, Pallas kernels, block_rows(): pl.pallas_call(block_kernel, out_shape=jax.ShapeDtypeStruct((ROWS, width)...  83.4 us
    pallas_call x1, Pallas kernels, token_table(): pl.pallas_call(table_kernel, out_shape=(jax.ShapeDtypeStruct((2 * PEERS,...  40.8 us
    unnamed x13, local copies, waits for them, and re-layouts  7.21 us

profile of v3, /device:TPU:0, one launch (start us, length us, event | category | flops | bytes accessed | tf_op | source)
XLA Modules:
  0.0 143.3 jit_solution(2696304263298860004)
XLA Ops:
  0.0 0.0 copy-start.4
  0.0 0.8 fusion
  0.8 0.8 select_reduce_fusion
  1.6 0.7 select_n.41
  2.3 0.7 copy.29
  3.0 0.1 reduce-window.8
  3.1 0.1 reduce
  3.2 0.7 sub.26
  3.9 0.1 select_reduce_fusion.1
  4.0 0.2 select_reduce_fusion.2
  4.1 0.6 broadcast_subtract_fusion
  4.7 0.8 reshape.83
  5.6 0.6 copy.39
  6.2 0.2 copy.32
  6.4 0.9 subtract_select_fusion.age_ref
  7.3 0.0 copy-done.4
  7.3 0.2 copy.35
  7.5 0.0 copy-start.3
  7.5 1.0 copy.36
  8.5 2.3 %constant_dynamic-slice_fusion.columns = bf16[512,1024]{1,0:T(8,128)(2,1)} fusion(bf16[512,4096]{1,0:T(8,128)(2,1)} %embed.1, s32[]{:T(128)S(6)} %select_n.44), kind=kLoop, calls=%fused_computation.12 | loop fusion | bytes 2097156 | tf_op jit(solution)/shard_map/dynamic_slice | solution.py:516
  10.8 0.0 copy-done.3
  10.8 0.7 copy.30
  11.5 0.0 copy-start
  11.5 0.1 copy.31
  11.6 0.0 copy-start.1
  11.6 0.1 dynamic-slice_bitcast_fusion.shares
  11.7 2.0 %copy-done = bf16[512,4096]{1,0:T(8,128)(2,1)S(1)} copy-done((bf16[512,4096]{1,0:T(8,128)(2,1)S(1)}, bf16[512,4096]{1,0:T(8,128)(2,1)}, u32[]{:S(2)}) %copy-start) | copy-done | bytes 4194328
  13.7 0.0 copy-done.1
  13.7 40.8 %shard_map.109 = (bf16[32,96,512]{2,1,0:T(8,128)(2,1)S(1)}, s32[6,128]{1,0:T(8,128)S(1)}) custom-call(bf16[16,96,256]{2,1,0:T(8,128)(2,1)S(1)} %dynamic-slice_bitcast_fusion.shares, bf16[512,4096]{1,0:T(8,128)(2,1)S(1)} %copy-done, f32[1,4096]{1,0:T(1,128)S(1)} %bitcast.20, s32[6,128]{1,0:T(8,128)S(1)} %bitcast.19), custom_call_target="tpu_custom_call" | custom-call | flops 402653184 | bytes 16777216 | tf_op jit(solution)/shard_map/pallas_call | solution.py:242
  54.4 0.0 copy-start.2
  54.4 1.7 %copy-done.2 = bf16[32,96,512]{2,1,0:T(8,128)(2,1)} copy-done((bf16[32,96,512]{2,1,0:T(8,128)(2,1)}, bf16[32,96,512]{2,1,0:T(8,128)(2,1)S(1)}, u32[]{:S(2)}) %copy-start.2) | copy-done | bytes 3145752
  56.1 0.1 slice.3
  56.2 0.1 pad_add_fusion
  56.2 1.0 copy.37.ids_ref
  57.3 83.4 %shard_map.110 = bf16[768,1024]{1,0:T(8,128)(2,1)} custom-call(s32[24]{0:T(128)} %get-tuple-element.12.begin_ref, s32[24]{0:T(128)} %get-tuple-element.11.end_ref, s32[912,1]{1,0:T(8,128)} %copy.37.ids_ref, s32[912,1]{1,0:T(8,128)} %subtract_select_fusion.age_ref, bf16[32,96,512]{2,1,0:T(8,128)(2,1)} %copy-done.2, f32[8,3,3,128]{3,2,1,0:T(4,128)} %bitcast.26, ...), custom_call_target="tpu_custom_call" | custom-call | flops 6442450944 | bytes 16777216 | tf_op jit(solution)/shard_map/pallas_call | solution.py:446
  140.7 2.7 %copy.41 = bf16[768,1024]{1,0:T(8,128)(2,1)} copy(bf16[768,1024]{1,0:T(8,128)(2,1)} %shard_map.110) | data formatting | bytes 3145728
  (2 shorter events, 0.0 us)
Async XLA Ops:
  0.0 7.3 %copy-start.4 = (f32[128,1024]{1,0:T(8,128)S(1)}, f32[128,1024]{1,0:T(8,128)}, u32[]{:S(2)}) copy-start(f32[128,1024]{1,0:T(8,128)} %param.19) | copy-start | bytes 1572868
  7.5 3.3 %copy-start.3 = (bf16[256,3,1024]{2,0,1:T(8,128)(2,1)S(1)}, bf16[256,3,1024]{2,0,1:T(8,128)(2,1)}, u32[]{:S(2)}) copy-start(bf16[256,3,1024]{2,0,1:T(8,128)(2,1)} %param.17) | copy-start | bytes 4718596
  11.5 2.2 %copy-start = (bf16[512,4096]{1,0:T(8,128)(2,1)S(1)}, bf16[512,4096]{1,0:T(8,128)(2,1)}, u32[]{:S(2)}) copy-start(bf16[512,4096]{1,0:T(8,128)(2,1)} %embed.1) | copy-start | bytes 12582916
  11.6 2.1 %copy-start.1 = (f32[4096]{0:T(1024)S(1)}, f32[4096]{0:T(1024)}, u32[]{:S(2)}) copy-start(f32[4096]{0:T(1024)} %param.16) | copy-start | bytes 49156
  54.4 1.7 %copy-start.2 = (bf16[32,96,512]{2,1,0:T(8,128)(2,1)}, bf16[32,96,512]{2,1,0:T(8,128)(2,1)S(1)}, u32[]{:S(2)}) copy-start(bf16[32,96,512]{2,1,0:T(8,128)(2,1)S(1)} %get-tuple-element.8.table) | copy-start | bytes 9437188

commit v4 on v3

--- a/solution.py
+++ b/solution.py
@@ -42,12 +42,12 @@
 
 
 class Ring:
-    def __init__(self, buffer, half, sent, come):
+    def __init__(self, buffer, low, rows, sent, come):
         d = lax.axis_index("dp")
         c = lax.axis_index("context")
         self.x, self.z, self.d = c // SIDE, lax.rem(c, SIDE), d
         self.buffer, self.sent, self.come = buffer, sent, come
-        self.low, self.high = pl.ds(0, half), pl.ds(half, half)
+        self.low, self.high = pl.ds(0, low), pl.ds(low, rows - low)
 
     def context(self, j, m):
         dx = (1 - self.d) * m + self.d * j
@@ -163,8 +163,6 @@
     come_w,
     sent_t,
     come_t,
-    sent_f,
-    come_f,
     ids_sem,
     local_sem,
 ):
@@ -211,34 +209,29 @@
         origin = moved(c, k, -1)
         total = total + product(got[origin], origin)
     piece[...] = total.astype(jnp.bfloat16)
-    mine = table.at[2 * c + d]
-    spread = [
-        send(piece, mine, sent_t.at[k], come_t.at[k], {"context": moved(c, k, 1)}) for k in range(1, PEERS)
-    ]
-    forward = [send(piece, mine, sent_f.at[0], come_f.at[0], other)]
-    forward[0].start()
-    for copy in spread:
-        copy.start()
-    local = pltpu.make_async_copy(piece, mine, local_sem)
+    local = pltpu.make_async_copy(piece, table.at[2 * c + d], local_sem)
     local.start()
-    for k in range(1, PEERS):
-        spread[k - 1].wait_recv()
-        slot = table.at[2 * moved(c, k, -1) + d]
-        forward.append(send(slot, slot, sent_f.at[k], come_f.at[k], other))
-        forward[k].start()
-    for copy in forward:
-        copy.wait_recv()
-    for copy in weights + spread + forward:
+    local.wait()
+    ring = Ring(table, SHARE * 2 // 3, SHARE, sent_t, come_t)
+    ring.hop1()
+    ring.cross((0, 0))
+    ring.hop2()
+    ring.hop3()
+    ring.hop4()
+    ring.hop5()
+    ring.crossed((0, 0), *Ring.set2, *Ring.set3, *Ring.set4, *Ring.set5)
+    for copy in weights:
         copy.wait_send()
+    ring.across(0, 0).wait_send()
+    ring.drain()
     ids_copy.wait()
-    local.wait()
 
 
 def token_table(shares, embed, gain, ids):
     vmem = pl.BlockSpec(memory_space=pltpu.VMEM)
     anywhere = pl.BlockSpec(memory_space=pl.ANY)
     vocab, width = embed.shape
-    semaphores = [pltpu.SemaphoreType.DMA((PEERS,))] * 6
+    semaphores = [pltpu.SemaphoreType.DMA((PEERS,))] * 2 + [pltpu.SemaphoreType.DMA((36,))] * 2
     return pl.pallas_call(
         table_kernel,
         out_shape=(
@@ -307,7 +300,7 @@
     local = [pltpu.make_async_copy(weight.at[h], weights.at[2 * c + h], local_sem.at[h]) for h in range(2)]
     for copy in local:
         copy.start()
-    outs = Ring(weights, LANES // 2, sent_w, come_w)
+    outs = Ring(weights, LANES // 2, LANES, sent_w, come_w)
 
     vocab = onehot.shape[1]
     ids = jnp.broadcast_to(ids_ref[...], (EXT, vocab))
@@ -341,7 +334,7 @@
             further[direction].start()
 
     def chunk(i, carry):
-        for at, hop in ((1, outs.hop2), (2, outs.hop3), (4, outs.hop4), (5, outs.hop5)):
+        for at, hop in ((1, outs.hop2), (3, outs.hop3), (5, outs.hop4), (6, outs.hop5)):
             pl.when(i == at)(hop)
 
         pieces = table[pl.ds(i * 4, 4)].reshape(3 * LANES, vocab)
@@ -349,8 +342,9 @@
             onehot[...], pieces, (((1,), (1,)), ((), ())), preferred_element_type=jnp.float32
         )
         tap_index = lax.broadcasted_iota(jnp.int32, (TAPS, LANES), 0).astype(jnp.float32)
-        taps[...] = filt_ref[i] * jnp.exp(-decay_ref[i] * tap_index)
-        filters = short_ref[i]
+        channels = pl.ds(pl.multiple_of(i * LANES, LANES), LANES)
+        taps[...] = filt_ref[:, channels] * jnp.exp(-decay_ref[:, channels] * tap_index)
+        filters = short_ref[:, :, channels]
 
         def mixed(g, low, count):
             lanes = slice(g * LANES, (g + 1) * LANES)
@@ -413,7 +407,6 @@
         return carry
 
     lax.fori_loop(0, CHUNKS, chunk, 0)
-    hand_on(CHUNKS - 1)
 
     total[...] = jnp.dot(onehot[HALO:, :], columns[...], preferred_element_type=jnp.float32)
     outs.crossed(*Ring.set2, *Ring.set3, *Ring.set4, *Ring.set5)
@@ -426,7 +419,9 @@
         total[...] += jnp.dot(features, rows, preferred_element_type=jnp.float32)
         return carry
 
-    lax.fori_loop(0, CHUNKS, finish, 0)
+    lax.fori_loop(0, CHUNKS // 2, finish, 0)
+    hand_on(CHUNKS - 1)
+    lax.fori_loop(CHUNKS // 2, CHUNKS, finish, 0)
     out_ref[...] = total[...].astype(jnp.bfloat16)
 
     def drain(i, carry):
@@ -520,9 +515,9 @@
         ids[:, None],
         age[:, None],
         table,
-        short_filter.reshape(3, 3, CHUNKS, LANES).transpose(2, 0, 1, 3),
-        mr_filter.reshape(TAPS, CHUNKS, LANES).transpose(1, 0, 2),
-        mr_decay.reshape(CHUNKS, 1, LANES),
+        short_filter,
+        mr_filter,
+        mr_decay[None, :],
         columns,
         out_weight.reshape(2, DEPTH // 2, width),
     )

time: 144 us -> 127 us (0.88)
  Pallas kernels: 124 us -> 111 us
  local copies, waits for them, and re-layouts: 14.1 us -> 11.5 us
    pallas_call x1, Pallas kernels: 83.4 us -> 74.3 us  [block_rows(): pl.pallas_call(block_kernel, out_shape=jax.ShapeDtypeStruct((ROWS, width)...]
    pallas_call x1, Pallas kernels: 40.8 us -> 36.4 us  [token_table(): pl.pallas_call(table_kernel, out_shape=(jax.ShapeDtypeStruct((2 * PEERS,...]
    reshape x3 -> x0, local copies, waits for them, and re-layouts: 2.47 us -> none  [the longest x2 1.45 us: body(): short_filter.reshape(3, 3, CHUNKS, LANES).transpose(2, 0, 1, 3)]
    unnamed x13 -> x10, local copies, waits for them, and re-layouts: 7.21 us -> 7.01 us
where the time goes in v4:
time: 127 us
  Pallas kernels  111 us (87%)
  local copies, waits for them, and re-layouts  11.5 us (9%)
  other arithmetic  4.87 us (4%)
    pallas_call x1, Pallas kernels, block_rows(): pl.pallas_call(block_kernel, out_shape=jax.ShapeDtypeStruct((ROWS, width)...  74.3 us
    pallas_call x1, Pallas kernels, token_table(): pl.pallas_call(table_kernel, out_shape=(jax.ShapeDtypeStruct((2 * PEERS,...  36.4 us
    unnamed x10, local copies, waits for them, and re-layouts  7.01 us

profile of v4, /device:TPU:0, one launch (start us, length us, event | category | flops | bytes accessed | tf_op | source)
XLA Modules:
  0.0 127.2 jit_solution(16067659580735722641)
XLA Ops:
  0.0 0.8 fusion
  0.8 0.8 select_reduce_fusion
  1.5 0.7 select_n.41
  2.2 0.7 copy.23
  3.0 0.1 reduce-window.8
  3.0 0.1 reduce
  3.1 0.7 sub.26
  3.8 0.1 select_reduce_fusion.1
  3.9 0.2 select_reduce_fusion.2
  4.1 0.6 broadcast_subtract_fusion
  4.7 0.2 copy.26
  4.9 0.0 copy-start.3
  4.9 0.9 subtract_select_fusion.age_ref
  5.8 2.3 %constant_dynamic-slice_fusion.columns = bf16[512,1024]{1,0:T(8,128)(2,1)} fusion(bf16[512,4096]{1,0:T(8,128)(2,1)} %embed.1, s32[]{:T(128)S(6)} %select_n.44), kind=kLoop, calls=%fused_computation.11 | loop fusion | bytes 2097156 | tf_op jit(solution)/shard_map/dynamic_slice | solution.py:511
  8.0 0.0 copy-done.3
  8.0 0.7 copy.24
  8.7 0.0 copy-start
  8.8 0.1 copy.25
  8.9 0.0 copy-start.1
  8.9 0.1 dynamic-slice_bitcast_fusion.shares
  8.9 2.0 %copy-done = bf16[512,4096]{1,0:T(8,128)(2,1)S(1)} copy-done((bf16[512,4096]{1,0:T(8,128)(2,1)S(1)}, bf16[512,4096]{1,0:T(8,128)(2,1)}, u32[]{:S(2)}) %copy-start) | copy-done | bytes 4194328
  10.9 0.0 copy-done.1
  10.9 36.4 %shard_map.109 = (bf16[32,96,512]{2,1,0:T(8,128)(2,1)S(1)}, s32[6,128]{1,0:T(8,128)S(1)}) custom-call(bf16[16,96,256]{2,1,0:T(8,128)(2,1)S(1)} %dynamic-slice_bitcast_fusion.shares, bf16[512,4096]{1,0:T(8,128)(2,1)S(1)} %copy-done, f32[1,4096]{1,0:T(1,128)S(1)} %bitcast.15, s32[6,128]{1,0:T(8,128)S(1)} %bitcast.14), custom_call_target="tpu_custom_call" | custom-call | flops 402653184 | bytes 16777216 | tf_op jit(solution)/shard_map/pallas_call | solution.py:235
  47.4 0.0 copy-start.2
  47.4 1.7 %copy-done.2 = bf16[32,96,512]{2,1,0:T(8,128)(2,1)} copy-done((bf16[32,96,512]{2,1,0:T(8,128)(2,1)}, bf16[32,96,512]{2,1,0:T(8,128)(2,1)S(1)}, u32[]{:S(2)}) %copy-start.2) | copy-done | bytes 3145752
  49.1 0.1 slice.3
  49.1 0.1 pad_add_fusion
  49.2 1.0 copy.28.ids_ref
  50.2 74.3 %shard_map.110 = bf16[768,1024]{1,0:T(8,128)(2,1)} custom-call(s32[24]{0:T(128)} %get-tuple-element.12.begin_ref, s32[24]{0:T(128)} %get-tuple-element.11.end_ref, s32[912,1]{1,0:T(8,128)} %copy.28.ids_ref, s32[912,1]{1,0:T(8,128)} %subtract_select_fusion.age_ref, bf16[32,96,512]{2,1,0:T(8,128)(2,1)} %copy-done.2, f32[3,3,1024]{2,1,0:T(4,128)} %short_ref.1, ...), custom_call_target="tpu_custom_call" | custom-call | flops 6442450944 | bytes 16777216 | tf_op jit(solution)/shard_map/pallas_call | solution.py:441
  124.5 2.7 %copy.30 = bf16[768,1024]{1,0:T(8,128)(2,1)} copy(bf16[768,1024]{1,0:T(8,128)(2,1)} %shard_map.110) | data formatting | bytes 3145728
  (2 shorter events, 0.0 us)
Async XLA Ops:
  4.9 3.1 %copy-start.3 = (bf16[256,3,1024]{2,0,1:T(8,128)(2,1)S(1)}, bf16[256,3,1024]{2,0,1:T(8,128)(2,1)}, u32[]{:S(2)}) copy-start(bf16[256,3,1024]{2,0,1:T(8,128)(2,1)} %param.17) | copy-start | bytes 4718596
  8.7 2.2 %copy-start = (bf16[512,4096]{1,0:T(8,128)(2,1)S(1)}, bf16[512,4096]{1,0:T(8,128)(2,1)}, u32[]{:S(2)}) copy-start(bf16[512,4096]{1,0:T(8,128)(2,1)} %embed.1) | copy-start | bytes 12582916
  8.9 2.1 %copy-start.1 = (f32[4096]{0:T(1024)S(1)}, f32[4096]{0:T(1024)}, u32[]{:S(2)}) copy-start(f32[4096]{0:T(1024)} %param.16) | copy-start | bytes 49156
  47.4 1.7 %copy-start.2 = (bf16[32,96,512]{2,1,0:T(8,128)(2,1)}, bf16[32,96,512]{2,1,0:T(8,128)(2,1)S(1)}, u32[]{:S(2)}) copy-start(bf16[32,96,512]{2,1,0:T(8,128)(2,1)S(1)} %get-tuple-element.8.table) | copy-start | bytes 9437188

commit v5 on v4

--- a/solution.py
+++ b/solution.py
@@ -28,6 +28,12 @@
     return x * SIDE + z
 
 
+def tree_sum(terms):
+    while len(terms) > 1:
+        terms = [sum(terms[k + 1 : k + 2], terms[k]) for k in range(0, len(terms), 2)]
+    return terms[0]
+
+
 def greet(axis_targets):
     barrier = pltpu.get_barrier_semaphore()
     for target in axis_targets:
@@ -156,7 +162,9 @@
     ids,
     table,
     before,
+    columns,
     got,
+    wide,
     normed,
     piece,
     sent_w,
@@ -165,9 +173,12 @@
     come_t,
     ids_sem,
     local_sem,
+    embed_sem,
 ):
     d = lax.axis_index("dp")
     c = lax.axis_index("context")
+    local_embed = pltpu.make_async_copy(embed, wide, embed_sem)
+    local_embed.start()
     other = {"dp": 1 - d}
     following = lax.rem(c + 1, PEERS)
     previous = lax.rem(c + PEERS - 1, PEERS)
@@ -184,19 +195,23 @@
     ids_copy = send(ids, before, ids_sem.at[0], ids_sem.at[1], {"context": following})
     ids_copy.start()
 
+    local_embed.wait()
     vocab, width = embed.shape
     step = 32
 
     def norm_rows(i, carry):
         rows = pl.ds(pl.multiple_of(i * step, step), step)
-        wide = embed[rows, :].astype(jnp.float32)
-        scale = lax.rsqrt(jnp.mean(wide * wide, axis=1, keepdims=True) + 1e-06)
-        values = (wide * scale * gain[...]).astype(jnp.bfloat16)
+        values = wide[rows, :].astype(jnp.float32)
+        scale = lax.rsqrt(jnp.mean(values * values, axis=1, keepdims=True) + 1e-06)
+        values = (values * scale * gain[...]).astype(jnp.bfloat16)
         for s in range(PEERS):
             normed[s, rows, :] = values[:, s * DEPTH : (s + 1) * DEPTH]
         return carry
 
     lax.fori_loop(0, vocab // step, norm_rows, 0)
+
+    own = pl.ds(pl.multiple_of(lax.axis_index("tensor") * columns.shape[1], LANES), columns.shape[1])
+    columns[...] = wide[:, own]
 
     def product(weight, s):
         return lax.dot_general(
@@ -237,15 +252,18 @@
         out_shape=(
             jax.ShapeDtypeStruct((2 * PEERS, SHARE, vocab), jnp.bfloat16),
             jax.ShapeDtypeStruct(ids.shape, jnp.int32),
+            jax.ShapeDtypeStruct((vocab, width // SIDE), jnp.bfloat16),
         ),
-        in_specs=[vmem, vmem, vmem, anywhere],
-        out_specs=(anywhere, anywhere),
+        in_specs=[vmem, anywhere, vmem, anywhere],
+        out_specs=(anywhere, anywhere, vmem),
         scratch_shapes=[
             pltpu.VMEM((PEERS, SHARE, DEPTH), jnp.bfloat16),
+            pltpu.VMEM((vocab, width), jnp.bfloat16),
             pltpu.VMEM((PEERS, vocab, DEPTH), jnp.bfloat16),
             pltpu.VMEM((SHARE, vocab), jnp.bfloat16),
             *semaphores,
             pltpu.SemaphoreType.DMA((2,)),
+            pltpu.SemaphoreType.DMA,
             pltpu.SemaphoreType.DMA,
         ],
         compiler_params=pltpu.CompilerParams(
@@ -256,17 +274,16 @@
 
 
 def block_kernel(
-    begin_ref,
-    end_ref,
     ids_ref,
     age_ref,
-    table,
+    table_in,
     short_ref,
     filt_ref,
     decay_ref,
     columns,
     weight,
     out_ref,
+    table,
     onehot,
     mask1,
     mask2,
@@ -293,6 +310,8 @@
     right = lax.rem(t + 1, SIDE)
     left = lax.rem(t + SIDE - 1, SIDE)
     other = {"dp": 1 - d}
+    local_table = pltpu.make_async_copy(table_in, table, local_sem.at[2])
+    local_table.start()
     greet(
         [{"tensor": right}, {"tensor": left}, other]
         + [{"context": moved(c, k, 1)} for k in range(1, PEERS)]
@@ -312,6 +331,7 @@
     for copy in local:
         copy.wait()
     outs.hop1()
+    local_table.wait()
 
     def own_copies(i):
         return (
@@ -343,7 +363,9 @@
         )
         tap_index = lax.broadcasted_iota(jnp.int32, (TAPS, LANES), 0).astype(jnp.float32)
         channels = pl.ds(pl.multiple_of(i * LANES, LANES), LANES)
-        taps[...] = filt_ref[:, channels] * jnp.exp(-decay_ref[:, channels] * tap_index)
+        values = filt_ref[:, channels] * jnp.exp(-decay_ref[:, channels] * tap_index)
+        for j in range(TAPS):
+            taps[j] = jnp.broadcast_to(values[j : j + 1], (8, LANES))
         filters = short_ref[:, :, channels]
 
         def mixed(g, low, count):
@@ -360,20 +382,16 @@
 
         def piece(n, carry):
             row = pl.multiple_of(HALO + n * R, 16)
-            begin = begin_ref[n]
-            end = end_ref[n]
+            head = row - jnp.broadcast_to(age_ref[pl.ds(row, 1), :], (TAPS, LANES))
             before = row - TAPS + lax.broadcasted_iota(jnp.int32, (TAPS, LANES), 0)
-            window[...] = jnp.where(before >= begin, prod[pl.ds(row - TAPS, TAPS), :], 0.0)
+            window[...] = jnp.where(before >= head, prod[pl.ds(row - TAPS, TAPS), :], 0.0)
             recent[...] = prod[pl.ds(row - 8, R + 8), :]
             age = jnp.broadcast_to(age_ref[pl.ds(row, R), :], (R, LANES))
             sums = [jnp.zeros((8, LANES), jnp.float32) for _ in range(R // 8)]
             near = [jnp.zeros((8, LANES), jnp.float32) for _ in range(R // 8)]
             for phase in range(8):
                 for block in range(0, TAPS // 8, GROUP):
-                    held = [
-                        jnp.broadcast_to(taps[pl.ds(phase + 8 * (block + m), 1), :], (8, LANES))
-                        for m in range(GROUP)
-                    ]
+                    held = [taps[phase + 8 * (block + m)] for m in range(GROUP)]
                     views = {
                         q: window[pl.ds(TAPS + 8 * q - phase, 8), :]
                         if q < 0
@@ -381,14 +399,19 @@
                         for q in range(-(block + GROUP - 1), R // 8 - block)
                     }
                     for i in range(R // 8):
+                        far, close = [], []
                         for m in range(GROUP):
                             q = i - block - m
                             if q < 0:
-                                sums[i] = sums[i] + held[m] * views[q]
+                                far.append(held[m] * views[q])
                             else:
                                 kept = age[8 * i : 8 * i + 8] >= phase + 8 * (block + m)
-                                near[i] = near[i] + held[m] * jnp.where(kept, views[q], 0.0)
-            mine = row + lax.broadcasted_iota(jnp.int32, (R, LANES), 0) < end
+                                close.append(held[m] * jnp.where(kept, views[q], 0.0))
+                        if far:
+                            sums[i] = sums[i] + tree_sum(far)
+                        if close:
+                            near[i] = near[i] + tree_sum(close)
+            mine = row + lax.broadcasted_iota(jnp.int32, (R, LANES), 0) - age == head[:R]
             result = jnp.where(mine, jnp.concatenate(sums, axis=0), 0.0) + jnp.concatenate(near, axis=0)
             longs[pl.ds(pl.multiple_of(n * R, R), R), :] = result
             return carry
@@ -433,17 +456,18 @@
     outs.drain()
 
 
-def block_rows(begin, end, ids, age, table, short_filter, mr_filter, mr_decay, columns, weight):
+def block_rows(ids, age, table, short_filter, mr_filter, mr_decay, columns, weight):
     vocab = table.shape[2]
     width = columns.shape[1]
-    smem = pl.BlockSpec(memory_space=pltpu.SMEM)
     vmem = pl.BlockSpec(memory_space=pltpu.VMEM)
+    anywhere = pl.BlockSpec(memory_space=pl.ANY)
     return pl.pallas_call(
         block_kernel,
         out_shape=jax.ShapeDtypeStruct((ROWS, width), jnp.bfloat16),
-        in_specs=[smem, smem] + [vmem] * 8,
+        in_specs=[vmem] * 2 + [anywhere] + [vmem] * 4 + [anywhere],
         out_specs=vmem,
         scratch_shapes=[
+            pltpu.VMEM(table.shape, jnp.bfloat16),
             pltpu.VMEM((EXT, vocab), jnp.bfloat16),
             pltpu.VMEM((EXT, LANES), jnp.float32),
             pltpu.VMEM((EXT, LANES), jnp.float32),
@@ -451,7 +475,7 @@
             pltpu.VMEM((EXT, LANES), jnp.float32),
             pltpu.VMEM((TAPS, LANES), jnp.float32),
             pltpu.VMEM((R + 8, LANES), jnp.float32),
-            pltpu.VMEM((TAPS, LANES), jnp.float32),
+            pltpu.VMEM((TAPS, 8, LANES), jnp.float32),
             pltpu.VMEM((ROWS, LANES), jnp.float32),
             pltpu.VMEM((SIDE, CHUNKS, ROWS, LANES), jnp.bfloat16),
             pltpu.VMEM((ROWS, width), jnp.float32),
@@ -462,13 +486,13 @@
             pltpu.SemaphoreType.DMA((2, CHUNKS)),
             pltpu.SemaphoreType.DMA((36,)),
             pltpu.SemaphoreType.DMA((36,)),
-            pltpu.SemaphoreType.DMA((2,)),
+            pltpu.SemaphoreType.DMA((3,)),
         ],
         compiler_params=pltpu.CompilerParams(
             collective_id=1, has_side_effects=True, vmem_limit_bytes=56 * 2**20
         ),
         cost_estimate=pl.CostEstimate(flops=2 * ROWS * width * 4096, bytes_accessed=2**24, transcendentals=0),
-    )(begin, end, ids, age, table, short_filter, mr_filter, mr_decay, columns, weight)
+    )(ids, age, table, short_filter, mr_filter, mr_decay, columns, weight)
 
 
 def body(
@@ -489,29 +513,21 @@
     width = out_weight.shape[1]
 
     matches = subst_pos[:, None] == jnp.arange(row_count, dtype=jnp.int32)[None, :]
-    chosen = jnp.sum(jnp.where(matches, subst_base[:, None], 0), axis=0)
-    touched = jnp.any(matches, axis=0)
-    new_ids = jnp.where(touched, chosen, token_ids)
+    chosen = jnp.max(jnp.where(matches, subst_base[:, None], -1), axis=0)
+    new_ids = jnp.where(chosen >= 0, chosen, token_ids)
 
     shares = in_weight.reshape(DEPTH, 3, CHUNKS, LANES).transpose(2, 1, 3, 0).reshape(PEERS, 2, SHARE, DEPTH)
     shares = lax.dynamic_index_in_dim(shares, lax.axis_index("dp"), 1, keepdims=False)
-    table, before = token_table(shares, embed_table, norm_gain[None, :], new_ids.reshape(-1, LANES))
+    table, before, columns = token_table(shares, embed_table, norm_gain[None, :], new_ids.reshape(-1, LANES))
     ids = jnp.concatenate([before.reshape(-1)[row_count - HALO :], new_ids])
 
     first_row = lax.axis_index("context") * row_count - HALO
-    ends = jnp.cumsum(window_lengths)
-    starts = ends - window_lengths
+    windows = jnp.arange(window_lengths.shape[0], dtype=jnp.int32)
+    starts = jnp.sum(jnp.where(windows[None, :] < windows[:, None], window_lengths[None, :], 0), axis=1)
     positions = first_row + jnp.arange(EXT, dtype=jnp.int32)
     begins = jnp.max(jnp.where(starts[None, :] <= positions[:, None], starts[None, :], -1), axis=1)
     age = jnp.where(begins >= 0, positions - begins, -1)
-    heads = first_row + HALO + R * jnp.arange(PIECES, dtype=jnp.int32)
-    head_begin = jnp.max(jnp.where(starts[None, :] <= heads[:, None], starts[None, :], -1), axis=1)
-    head_end = jnp.min(jnp.where(ends[None, :] > heads[:, None], ends[None, :], 1 << 20), axis=1)
-
-    columns = lax.dynamic_slice_in_dim(embed_table, lax.axis_index("tensor") * width, width, 1)
     return block_rows(
-        head_begin - first_row,
-        head_end - first_row,
         ids[:, None],
         age[:, None],
         table,

time: 127 us -> 126 us (level)
  other arithmetic: 4.87 us -> 3.28 us
    dynamic_slice x1 -> x0, local copies, waits for them, and re-layouts: 2.26 us -> none  [body(): lax.dynamic_slice_in_dim(embed_table, lax.axis_index('tensor') * width, w...]
    unnamed x10, local copies, waits for them, and re-layouts: 7.01 us -> 8.99 us
where the time goes in v5:
time: 126 us
  Pallas kernels  112 us (89%)
  local copies, waits for them, and re-layouts  10.5 us (8%)
  other arithmetic  3.28 us (3%)
    pallas_call x1, Pallas kernels, block_rows(): pl.pallas_call(block_kernel, out_shape=jax.ShapeDtypeStruct((ROWS, width)...  75 us
    pallas_call x1, Pallas kernels, token_table(): pl.pallas_call(table_kernel, out_shape=(jax.ShapeDtypeStruct((2 * PEERS,...  36.8 us
    unnamed x10, local copies, waits for them, and re-layouts  8.99 us

profile of v5, /device:TPU:0, one launch (start us, length us, event | category | flops | bytes accessed | tf_op | source)
XLA Modules:
  0.0 125.6 jit_solution(10875326903086840000)
XLA Ops:
  0.0 0.8 select_reduce_fusion.2
  0.8 0.8 select_reduce_fusion
  1.5 0.7 compare_select_fusion
  2.2 0.1 select_reduce_fusion.1
  2.4 0.2 copy.22
  2.6 0.9 subtract_select_fusion.age_ref
  3.4 1.7 %copy.20 = bf16[256,3,1024]{0,2,1:T(8,128)(2,1)S(1)} copy(bf16[256,3,1024]{2,0,1:T(8,128)(2,1)} %param.17) | data formatting | bytes 3145728 | tf_op args[6]
  5.2 0.0 copy-start
  5.2 0.1 copy.21
  5.3 0.0 copy-start.1
  5.3 0.1 dynamic-slice_bitcast_fusion.shares
  5.4 2.0 %copy-done = bf16[512,4096]{1,0:T(8,128)(2,1)S(1)} copy-done((bf16[512,4096]{1,0:T(8,128)(2,1)S(1)}, bf16[512,4096]{1,0:T(8,128)(2,1)}, u32[]{:S(2)}) %copy-start) | copy-done | bytes 4194328
  7.3 0.0 copy-done.1
  7.3 36.8 %shard_map.109 = (bf16[32,96,512]{2,1,0:T(8,128)(2,1)S(1)}, s32[6,128]{1,0:T(8,128)S(1)}, bf16[512,1024]{1,0:T(8,128)(2,1)S(1)}) custom-call(bf16[16,96,256]{2,1,0:T(8,128)(2,1)S(1)} %dynamic-slice_bitcast_fusion.shares, bf16[512,4096]{1,0:T(8,128)(2,1)S(1)} %copy-done, f32[1,4096]{1,0:T(1,128)S(1)} %bitcast.14, s32[6,128]{1,0:T(8,128)S(1)} %bitcast.13), custom_call_target="tpu_custom_call" | custom-call | flops 402653184 | bytes 16777216 | tf_op jit(solution)/shard_map/pallas_call | solution.py:250
  44.2 0.0 copy-start.2
  44.2 1.7 %copy-done.2 = bf16[32,96,512]{2,1,0:T(8,128)(2,1)} copy-done((bf16[32,96,512]{2,1,0:T(8,128)(2,1)}, bf16[32,96,512]{2,1,0:T(8,128)(2,1)S(1)}, u32[]{:S(2)}) %copy-start.2) | copy-done | bytes 3145752
  45.8 0.0 copy-start.3
  45.8 1.0 copy-done.3
  46.8 0.1 slice.3
  46.9 0.1 pad_add_fusion
  47.0 1.0 copy.24.ids_ref
  48.0 75.0 %shard_map.110 = bf16[768,1024]{1,0:T(8,128)(2,1)} custom-call(s32[912,1]{1,0:T(8,128)} %copy.24.ids_ref, s32[912,1]{1,0:T(8,128)} %subtract_select_fusion.age_ref, bf16[32,96,512]{2,1,0:T(8,128)(2,1)} %copy-done.2, f32[3,3,1024]{2,1,0:T(4,128)} %short_ref.1, f32[128,1024]{1,0:T(8,128)} %filt_ref.1, f32[1,1024]{1,0:T(1,128)} %bitcast.21, ...), custom_call_target="tpu_custom_call" | custom-call | flops 6442450944 | bytes 16777216 | tf_op jit(solution)/shard_map/pallas_call | solution.py:464
  122.9 2.7 %copy.26 = bf16[768,1024]{1,0:T(8,128)(2,1)} copy(bf16[768,1024]{1,0:T(8,128)(2,1)} %shard_map.110) | data formatting | bytes 3145728
  (1 shorter events, 0.0 us)
Async XLA Ops:
  5.2 2.2 %copy-start = (bf16[512,4096]{1,0:T(8,128)(2,1)S(1)}, bf16[512,4096]{1,0:T(8,128)(2,1)}, u32[]{:S(2)}) copy-start(bf16[512,4096]{1,0:T(8,128)(2,1)} %embed.1) | copy-start | bytes 12582916
  5.3 2.1 %copy-start.1 = (f32[4096]{0:T(1024)S(1)}, f32[4096]{0:T(1024)}, u32[]{:S(2)}) copy-start(f32[4096]{0:T(1024)} %param.16) | copy-start | bytes 49156
  44.2 1.7 %copy-start.2 = (bf16[32,96,512]{2,1,0:T(8,128)(2,1)}, bf16[32,96,512]{2,1,0:T(8,128)(2,1)S(1)}, u32[]{:S(2)}) copy-start(bf16[32,96,512]{2,1,0:T(8,128)(2,1)S(1)} %get-tuple-element.9.table_in) | copy-start | bytes 9437188
  45.8 1.0 copy-start.3

commit v6 on v5

--- a/solution.py
+++ b/solution.py
@@ -289,8 +289,8 @@
     mask2,
     src,
     prod,
-    window,
-    recent,
+    windows,
+    recents,
     taps,
     longs,
     gates,
@@ -380,7 +380,7 @@
             product = mixed(1, low, 48) * mixed(2, low, 48)
             prod[pl.ds(low, 48), :] = product.astype(jnp.bfloat16).astype(jnp.float32)
 
-        def piece(n, carry):
+        def piece(n, window, recent):
             row = pl.multiple_of(HALO + n * R, 16)
             head = row - jnp.broadcast_to(age_ref[pl.ds(row, 1), :], (TAPS, LANES))
             before = row - TAPS + lax.broadcasted_iota(jnp.int32, (TAPS, LANES), 0)
@@ -414,9 +414,13 @@
             mine = row + lax.broadcasted_iota(jnp.int32, (R, LANES), 0) - age == head[:R]
             result = jnp.where(mine, jnp.concatenate(sums, axis=0), 0.0) + jnp.concatenate(near, axis=0)
             longs[pl.ds(pl.multiple_of(n * R, R), R), :] = result
+
+        def two_pieces(n, carry):
+            for k in range(2):
+                piece(2 * n + k, windows.at[k], recents.at[k])
             return carry
 
-        lax.fori_loop(0, PIECES, piece, 0)
+        lax.fori_loop(0, PIECES // 2, two_pieces, 0)
         for low in range(0, ROWS, 48):
             gated = mixed(0, HALO + low, 48) * longs[pl.ds(low, 48), :]
             gates[t, i, pl.ds(low, 48), :] = gated.astype(jnp.bfloat16)
@@ -473,8 +477,8 @@
             pltpu.VMEM((EXT, LANES), jnp.float32),
             pltpu.VMEM((EXT + 8, 3 * LANES), jnp.float32),
             pltpu.VMEM((EXT, LANES), jnp.float32),
-            pltpu.VMEM((TAPS, LANES), jnp.float32),
-            pltpu.VMEM((R + 8, LANES), jnp.float32),
+            pltpu.VMEM((2, TAPS, LANES), jnp.float32),
+            pltpu.VMEM((2, R + 8, LANES), jnp.float32),
             pltpu.VMEM((TAPS, 8, LANES), jnp.float32),
             pltpu.VMEM((ROWS, LANES), jnp.float32),
             pltpu.VMEM((SIDE, CHUNKS, ROWS, LANES), jnp.bfloat16),
@@ -489,7 +493,7 @@
             pltpu.SemaphoreType.DMA((3,)),
         ],
         compiler_params=pltpu.CompilerParams(
-            collective_id=1, has_side_effects=True, vmem_limit_bytes=56 * 2**20
+            collective_id=1, has_side_effects=True, vmem_limit_bytes=40 * 2**20
         ),
         cost_estimate=pl.CostEstimate(flops=2 * ROWS * width * 4096, bytes_accessed=2**24, transcendentals=0),
     )(ids, age, table, short_filter, mr_filter, mr_decay, columns, weight)

time: 126 us -> 120 us (0.952)
  Pallas kernels: 112 us -> 108 us
  local copies, waits for them, and re-layouts: 10.5 us -> 9.07 us
    pallas_call x1, Pallas kernels: 75 us -> 71.1 us  [block_rows(): pl.pallas_call(block_kernel, out_shape=jax.ShapeDtypeStruct((ROWS, width)...]
    unnamed x10 -> x18, local copies, waits for them, and re-layouts: 8.99 us -> 8.4 us
where the time goes in v6:
time: 120 us
  Pallas kernels  108 us (90%)
  local copies, waits for them, and re-layouts  9.07 us (8%)
  other arithmetic  2.5 us (2%)
    pallas_call x1, Pallas kernels, block_rows(): pl.pallas_call(block_kernel, out_shape=jax.ShapeDtypeStruct((ROWS, width)...  71.1 us
    pallas_call x1, Pallas kernels, token_table(): pl.pallas_call(table_kernel, out_shape=(jax.ShapeDtypeStruct((2 * PEERS,...  36.9 us
    unnamed x18, local copies, waits for them, and re-layouts  8.4 us

profile of v6, /device:TPU:0, one launch (start us, length us, event | category | flops | bytes accessed | tf_op | source)
XLA Modules:
  0.0 119.7 jit_solution(17402175611134185386)
XLA Ops:
  0.0 0.8 select_reduce_fusion.2
  0.8 0.8 select_reduce_fusion
  1.5 0.7 compare_select_fusion
  2.2 0.1 select_reduce_fusion.1
  2.4 0.2 copy.22
  2.6 0.1 subtract_select_fusion.age_ref
  2.7 1.7 %copy.20 = bf16[256,3,1024]{0,2,1:T(8,128)(2,1)S(1)} copy(bf16[256,3,1024]{2,0,1:T(8,128)(2,1)} %param.17) | data formatting | bytes 3145728 | tf_op args[6]
  4.4 0.0 copy-start
  4.4 0.1 copy.21
  4.5 0.0 copy-start.1
  4.5 0.1 dynamic-slice_bitcast_fusion.shares
  4.6 2.0 %copy-done = bf16[512,4096]{1,0:T(8,128)(2,1)S(1)} copy-done((bf16[512,4096]{1,0:T(8,128)(2,1)S(1)}, bf16[512,4096]{1,0:T(8,128)(2,1)}, u32[]{:S(2)}) %copy-start) | copy-done | bytes 4194328
  6.6 0.0 copy-done.1
  6.6 0.0 copy-start.4
  6.6 0.0 copy-start.5
  6.6 0.0 copy-start.6
  6.6 0.0 copy-start.7
  6.6 36.9 %shard_map.109 = (bf16[32,96,512]{2,1,0:T(8,128)(2,1)S(1)}, s32[6,128]{1,0:T(8,128)S(1)}, bf16[512,1024]{1,0:T(8,128)(2,1)S(1)}) custom-call(bf16[16,96,256]{2,1,0:T(8,128)(2,1)S(1)} %dynamic-slice_bitcast_fusion.shares, bf16[512,4096]{1,0:T(8,128)(2,1)S(1)} %copy-done, f32[1,4096]{1,0:T(1,128)S(1)} %bitcast.14, s32[6,128]{1,0:T(8,128)S(1)} %bitcast.13), custom_call_target="tpu_custom_call" | custom-call | flops 402653184 | bytes 16777216 | tf_op jit(solution)/shard_map/pallas_call | solution.py:250
  43.5 0.0 copy-start.2
  43.5 1.7 %copy-done.2 = bf16[32,96,512]{2,1,0:T(8,128)(2,1)} copy-done((bf16[32,96,512]{2,1,0:T(8,128)(2,1)}, bf16[32,96,512]{2,1,0:T(8,128)(2,1)S(1)}, u32[]{:S(2)}) %copy-start.2) | copy-done | bytes 3145752
  45.2 0.1 slice.3
  45.2 0.1 pad_add_fusion
  45.3 0.2 copy.24.ids_ref
  45.5 0.0 copy-done.4
  45.6 0.0 copy-done.5
  45.6 0.0 copy-done.6
  45.6 0.0 copy-done.7
  45.6 0.0 copy-start.3
  45.6 1.9 %copy-done.3 = bf16[32,96,512]{2,1,0:T(8,128)(2,1)S(1)} copy-done((bf16[32,96,512]{2,1,0:T(8,128)(2,1)S(1)}, bf16[32,96,512]{2,1,0:T(8,128)(2,1)}, u32[]{:S(2)}) %copy-start.3) | copy-done | bytes 3145752
  47.5 71.1 %shard_map.110 = bf16[768,1024]{1,0:T(8,128)(2,1)S(1)} custom-call(s32[912,1]{1,0:T(8,128)S(1)} %copy.24.ids_ref, s32[912,1]{1,0:T(8,128)S(1)} %subtract_select_fusion.age_ref, bf16[32,96,512]{2,1,0:T(8,128)(2,1)S(1)} %copy-done.3, f32[3,3,1024]{2,1,0:T(4,128)S(1)} %copy-done.6, f32[128,1024]{1,0:T(8,128)S(1)} %copy-done.4, f32[1,1024]{1,0:T(1,128)S(1)} %bitcast.17, ...), custom_call_target="tpu_custom_call" | custom-call | flops 6442450944 | bytes 16777216 | tf_op jit(solution)/shard_map/pallas_call | solution.py:468
  118.6 1.1 copy.26
  (1 shorter events, 0.0 us)
Async XLA Ops:
  4.4 2.2 %copy-start = (bf16[512,4096]{1,0:T(8,128)(2,1)S(1)}, bf16[512,4096]{1,0:T(8,128)(2,1)}, u32[]{:S(2)}) copy-start(bf16[512,4096]{1,0:T(8,128)(2,1)} %embed.1) | copy-start | bytes 12582916
  4.5 2.1 %copy-start.1 = (f32[4096]{0:T(1024)S(1)}, f32[4096]{0:T(1024)}, u32[]{:S(2)}) copy-start(f32[4096]{0:T(1024)} %param.16) | copy-start | bytes 49156
  6.6 39.0 %copy-start.4 = (f32[128,1024]{1,0:T(8,128)S(1)}, f32[128,1024]{1,0:T(8,128)}, u32[]{:S(2)}) copy-start(f32[128,1024]{1,0:T(8,128)} %filt_ref.1) | copy-start | bytes 1572868
  6.6 39.0 %copy-start.5 = (bf16[256,1024]{1,0:T(8,128)(2,1)S(1)}, bf16[256,1024]{1,0:T(8,128)(2,1)}, u32[]{:S(2)}) copy-start(bf16[256,1024]{1,0:T(8,128)(2,1)} %param.21) | copy-start | bytes 1572868
  6.6 39.0 %copy-start.6 = (f32[3,3,1024]{2,1,0:T(4,128)S(1)}, f32[3,3,1024]{2,1,0:T(4,128)}, u32[]{:S(2)}) copy-start(f32[3,3,1024]{2,1,0:T(4,128)} %short_ref.1) | copy-start | bytes 110596
  6.6 39.0 %copy-start.7 = (f32[1024]{0:T(1024)S(1)}, f32[1024]{0:T(1024)}, u32[]{:S(2)}) copy-start(f32[1024]{0:T(1024)} %param.20) | copy-start | bytes 12292
  43.5 1.7 %copy-start.2 = (bf16[32,96,512]{2,1,0:T(8,128)(2,1)}, bf16[32,96,512]{2,1,0:T(8,128)(2,1)S(1)}, u32[]{:S(2)}) copy-start(bf16[32,96,512]{2,1,0:T(8,128)(2,1)S(1)} %get-tuple-element.9.table_in) | copy-start | bytes 9437188
  45.6 1.9 %copy-start.3 = (bf16[32,96,512]{2,1,0:T(8,128)(2,1)S(1)}, bf16[32,96,512]{2,1,0:T(8,128)(2,1)}, u32[]{:S(2)}) copy-start(bf16[32,96,512]{2,1,0:T(8,128)(2,1)} %copy-done.2) | copy-start | bytes 9437188

commit v7 on v6

--- a/solution.py
+++ b/solution.py
@@ -405,8 +405,9 @@
                             if q < 0:
                                 far.append(held[m] * views[q])
                             else:
-                                kept = age[8 * i : 8 * i + 8] >= phase + 8 * (block + m)
-                                close.append(held[m] * jnp.where(kept, views[q], 0.0))
+                                tap = phase + 8 * (block + m)
+                                kept = age[8 * i : 8 * i + 8] >= tap
+                                close.append(held[m] * (jnp.where(kept, views[q], 0.0) if tap else views[q]))
                         if far:
                             sums[i] = sums[i] + tree_sum(far)
                         if close:
@@ -416,6 +417,10 @@
             longs[pl.ds(pl.multiple_of(n * R, R), R), :] = result
 
         def two_pieces(n, carry):
+            @pl.when((i > 0) & (n == PIECES // 4))
+            def _():
+                hand_on(i - 1)
+
             for k in range(2):
                 piece(2 * n + k, windows.at[k], recents.at[k])
             return carry
@@ -426,10 +431,6 @@
             gates[t, i, pl.ds(low, 48), :] = gated.astype(jnp.bfloat16)
         for copy in own_copies(i):
             copy.start()
-
-        @pl.when(i > 0)
-        def _():
-            hand_on(i - 1)
 
         return carry
 

time: 120 us -> 135 us (1.12)
  Pallas kernels: 108 us -> 123 us
    pallas_call x1, Pallas kernels: 71.1 us -> 86.3 us  [block_rows(): pl.pallas_call(block_kernel, out_shape=jax.ShapeDtypeStruct((ROWS, width)...]
where the time goes in v7:
time: 135 us
  Pallas kernels  123 us (91%)
  local copies, waits for them, and re-layouts  9.07 us (7%)
  other arithmetic  2.5 us (2%)
    pallas_call x1, Pallas kernels, block_rows(): pl.pallas_call(block_kernel, out_shape=jax.ShapeDtypeStruct((ROWS, width)...  86.3 us
    pallas_call x1, Pallas kernels, token_table(): pl.pallas_call(table_kernel, out_shape=(jax.ShapeDtypeStruct((2 * PEERS,...  36.9 us
    unnamed x18, local copies, waits for them, and re-layouts  8.4 us

profile of v7, /device:TPU:0, one launch (start us, length us, event | category | flops | bytes accessed | tf_op | source)
XLA Modules:
  0.0 134.9 jit_solution(10998265930202990907)
XLA Ops:
  0.0 0.8 select_reduce_fusion.2
  0.8 0.8 select_reduce_fusion
  1.5 0.7 compare_select_fusion
  2.2 0.1 select_reduce_fusion.1
  2.4 0.2 copy.22
  2.6 0.1 subtract_select_fusion.age_ref
  2.7 1.7 %copy.20 = bf16[256,3,1024]{0,2,1:T(8,128)(2,1)S(1)} copy(bf16[256,3,1024]{2,0,1:T(8,128)(2,1)} %param.17) | data formatting | bytes 3145728 | tf_op args[6]
  4.4 0.0 copy-start
  4.4 0.1 copy.21
  4.5 0.0 copy-start.1
  4.5 0.1 dynamic-slice_bitcast_fusion.shares
  4.6 2.0 %copy-done = bf16[512,4096]{1,0:T(8,128)(2,1)S(1)} copy-done((bf16[512,4096]{1,0:T(8,128)(2,1)S(1)}, bf16[512,4096]{1,0:T(8,128)(2,1)}, u32[]{:S(2)}) %copy-start) | copy-done | bytes 4194328
  6.6 0.0 copy-done.1
  6.6 0.0 copy-start.4
  6.6 0.0 copy-start.5
  6.6 0.0 copy-start.6
  6.6 0.0 copy-start.7
  6.6 36.9 %shard_map.109 = (bf16[32,96,512]{2,1,0:T(8,128)(2,1)S(1)}, s32[6,128]{1,0:T(8,128)S(1)}, bf16[512,1024]{1,0:T(8,128)(2,1)S(1)}) custom-call(bf16[16,96,256]{2,1,0:T(8,128)(2,1)S(1)} %dynamic-slice_bitcast_fusion.shares, bf16[512,4096]{1,0:T(8,128)(2,1)S(1)} %copy-done, f32[1,4096]{1,0:T(1,128)S(1)} %bitcast.14, s32[6,128]{1,0:T(8,128)S(1)} %bitcast.13), custom_call_target="tpu_custom_call" | custom-call | flops 402653184 | bytes 16777216 | tf_op jit(solution)/shard_map/pallas_call | solution.py:250
  43.5 0.0 copy-start.2
  43.5 1.7 %copy-done.2 = bf16[32,96,512]{2,1,0:T(8,128)(2,1)} copy-done((bf16[32,96,512]{2,1,0:T(8,128)(2,1)}, bf16[32,96,512]{2,1,0:T(8,128)(2,1)S(1)}, u32[]{:S(2)}) %copy-start.2) | copy-done | bytes 3145752
  45.2 0.1 slice.3
  45.2 0.1 pad_add_fusion
  45.3 0.2 copy.24.ids_ref
  45.5 0.0 copy-done.4
  45.6 0.0 copy-done.5
  45.6 0.0 copy-done.6
  45.6 0.0 copy-done.7
  45.6 0.0 copy-start.3
  45.6 1.9 %copy-done.3 = bf16[32,96,512]{2,1,0:T(8,128)(2,1)S(1)} copy-done((bf16[32,96,512]{2,1,0:T(8,128)(2,1)S(1)}, bf16[32,96,512]{2,1,0:T(8,128)(2,1)}, u32[]{:S(2)}) %copy-start.3) | copy-done | bytes 3145752
  47.5 86.3 %shard_map.110 = bf16[768,1024]{1,0:T(8,128)(2,1)S(1)} custom-call(s32[912,1]{1,0:T(8,128)S(1)} %copy.24.ids_ref, s32[912,1]{1,0:T(8,128)S(1)} %subtract_select_fusion.age_ref, bf16[32,96,512]{2,1,0:T(8,128)(2,1)S(1)} %copy-done.3, f32[3,3,1024]{2,1,0:T(4,128)S(1)} %copy-done.6, f32[128,1024]{1,0:T(8,128)S(1)} %copy-done.4, f32[1,1024]{1,0:T(1,128)S(1)} %bitcast.17, ...), custom_call_target="tpu_custom_call" | custom-call | flops 6442450944 | bytes 16777216 | tf_op jit(solution)/shard_map/pallas_call | solution.py:469
  133.8 1.1 copy.26
  (1 shorter events, 0.0 us)
Async XLA Ops:
  4.4 2.2 %copy-start = (bf16[512,4096]{1,0:T(8,128)(2,1)S(1)}, bf16[512,4096]{1,0:T(8,128)(2,1)}, u32[]{:S(2)}) copy-start(bf16[512,4096]{1,0:T(8,128)(2,1)} %embed.1) | copy-start | bytes 12582916
  4.5 2.1 %copy-start.1 = (f32[4096]{0:T(1024)S(1)}, f32[4096]{0:T(1024)}, u32[]{:S(2)}) copy-start(f32[4096]{0:T(1024)} %param.16) | copy-start | bytes 49156
  6.6 39.0 %copy-start.4 = (f32[128,1024]{1,0:T(8,128)S(1)}, f32[128,1024]{1,0:T(8,128)}, u32[]{:S(2)}) copy-start(f32[128,1024]{1,0:T(8,128)} %filt_ref.1) | copy-start | bytes 1572868
  6.6 39.0 %copy-start.5 = (bf16[256,1024]{1,0:T(8,128)(2,1)S(1)}, bf16[256,1024]{1,0:T(8,128)(2,1)}, u32[]{:S(2)}) copy-start(bf16[256,1024]{1,0:T(8,128)(2,1)} %param.21) | copy-start | bytes 1572868
  6.6 39.0 %copy-start.6 = (f32[3,3,1024]{2,1,0:T(4,128)S(1)}, f32[3,3,1024]{2,1,0:T(4,128)}, u32[]{:S(2)}) copy-start(f32[3,3,1024]{2,1,0:T(4,128)} %short_ref.1) | copy-start | bytes 110596
  6.6 39.0 %copy-start.7 = (f32[1024]{0:T(1024)S(1)}, f32[1024]{0:T(1024)}, u32[]{:S(2)}) copy-start(f32[1024]{0:T(1024)} %param.20) | copy-start | bytes 12292
  43.5 1.7 %copy-start.2 = (bf16[32,96,512]{2,1,0:T(8,128)(2,1)}, bf16[32,96,512]{2,1,0:T(8,128)(2,1)S(1)}, u32[]{:S(2)}) copy-start(bf16[32,96,512]{2,1,0:T(8,128)(2,1)S(1)} %get-tuple-element.9.table_in) | copy-start | bytes 9437188
  45.6 1.9 %copy-start.3 = (bf16[32,96,512]{2,1,0:T(8,128)(2,1)S(1)}, bf16[32,96,512]{2,1,0:T(8,128)(2,1)}, u32[]{:S(2)}) copy-start(bf16[32,96,512]{2,1,0:T(8,128)(2,1)} %copy-done.2) | copy-start | bytes 9437188

commit v8 on v6

--- a/solution.py
+++ b/solution.py
@@ -354,7 +354,7 @@
             further[direction].start()
 
     def chunk(i, carry):
-        for at, hop in ((1, outs.hop2), (3, outs.hop3), (5, outs.hop4), (6, outs.hop5)):
+        for at, hop in ((2, outs.hop2), (4, outs.hop3), (6, outs.hop4), (7, outs.hop5)):
             pl.when(i == at)(hop)
 
         pieces = table[pl.ds(i * 4, 4)].reshape(3 * LANES, vocab)

time: 120 us -> 117 us (0.975)
  Pallas kernels: 108 us -> 105 us
    pallas_call x1, Pallas kernels: 71.1 us -> 68.6 us  [block_rows(): pl.pallas_call(block_kernel, out_shape=jax.ShapeDtypeStruct((ROWS, width)...]
where the time goes in v8:
time: 117 us
  Pallas kernels  105 us (90%)
  local copies, waits for them, and re-layouts  9.07 us (8%)
  other arithmetic  2.5 us (2%)
    pallas_call x1, Pallas kernels, block_rows(): pl.pallas_call(block_kernel, out_shape=jax.ShapeDtypeStruct((ROWS, width)...  68.6 us
    pallas_call x1, Pallas kernels, token_table(): pl.pallas_call(table_kernel, out_shape=(jax.ShapeDtypeStruct((2 * PEERS,...  36.9 us
    unnamed x18, local copies, waits for them, and re-layouts  8.4 us

profile of v8, /device:TPU:0, one launch (start us, length us, event | category | flops | bytes accessed | tf_op | source)
XLA Modules:
  0.0 117.2 jit_solution(7382736183324687916)
XLA Ops:
  0.0 0.8 select_reduce_fusion.2
  0.8 0.8 select_reduce_fusion
  1.5 0.7 compare_select_fusion
  2.2 0.1 select_reduce_fusion.1
  2.4 0.2 copy.22
  2.6 0.1 subtract_select_fusion.age_ref
  2.7 1.7 %copy.20 = bf16[256,3,1024]{0,2,1:T(8,128)(2,1)S(1)} copy(bf16[256,3,1024]{2,0,1:T(8,128)(2,1)} %param.17) | data formatting | bytes 3145728 | tf_op args[6]
  4.4 0.0 copy-start
  4.4 0.1 copy.21
  4.5 0.0 copy-start.1
  4.5 0.1 dynamic-slice_bitcast_fusion.shares
  4.6 2.0 %copy-done = bf16[512,4096]{1,0:T(8,128)(2,1)S(1)} copy-done((bf16[512,4096]{1,0:T(8,128)(2,1)S(1)}, bf16[512,4096]{1,0:T(8,128)(2,1)}, u32[]{:S(2)}) %copy-start) | copy-done | bytes 4194328
  6.6 0.0 copy-done.1
  6.6 0.0 copy-start.4
  6.6 0.0 copy-start.5
  6.6 0.0 copy-start.6
  6.6 0.0 copy-start.7
  6.6 36.9 %shard_map.109 = (bf16[32,96,512]{2,1,0:T(8,128)(2,1)S(1)}, s32[6,128]{1,0:T(8,128)S(1)}, bf16[512,1024]{1,0:T(8,128)(2,1)S(1)}) custom-call(bf16[16,96,256]{2,1,0:T(8,128)(2,1)S(1)} %dynamic-slice_bitcast_fusion.shares, bf16[512,4096]{1,0:T(8,128)(2,1)S(1)} %copy-done, f32[1,4096]{1,0:T(1,128)S(1)} %bitcast.14, s32[6,128]{1,0:T(8,128)S(1)} %bitcast.13), custom_call_target="tpu_custom_call" | custom-call | flops 402653184 | bytes 16777216 | tf_op jit(solution)/shard_map/pallas_call | solution.py:250
  43.5 0.0 copy-start.2
  43.5 1.7 %copy-done.2 = bf16[32,96,512]{2,1,0:T(8,128)(2,1)} copy-done((bf16[32,96,512]{2,1,0:T(8,128)(2,1)}, bf16[32,96,512]{2,1,0:T(8,128)(2,1)S(1)}, u32[]{:S(2)}) %copy-start.2) | copy-done | bytes 3145752
  45.2 0.1 slice.3
  45.2 0.1 pad_add_fusion
  45.3 0.2 copy.24.ids_ref
  45.5 0.0 copy-done.4
  45.6 0.0 copy-done.5
  45.6 0.0 copy-done.6
  45.6 0.0 copy-done.7
  45.6 0.0 copy-start.3
  45.6 1.9 %copy-done.3 = bf16[32,96,512]{2,1,0:T(8,128)(2,1)S(1)} copy-done((bf16[32,96,512]{2,1,0:T(8,128)(2,1)S(1)}, bf16[32,96,512]{2,1,0:T(8,128)(2,1)}, u32[]{:S(2)}) %copy-start.3) | copy-done | bytes 3145752
  47.5 68.6 %shard_map.110 = bf16[768,1024]{1,0:T(8,128)(2,1)S(1)} custom-call(s32[912,1]{1,0:T(8,128)S(1)} %copy.24.ids_ref, s32[912,1]{1,0:T(8,128)S(1)} %subtract_select_fusion.age_ref, bf16[32,96,512]{2,1,0:T(8,128)(2,1)S(1)} %copy-done.3, f32[3,3,1024]{2,1,0:T(4,128)S(1)} %copy-done.6, f32[128,1024]{1,0:T(8,128)S(1)} %copy-done.4, f32[1,1024]{1,0:T(1,128)S(1)} %bitcast.17, ...), custom_call_target="tpu_custom_call" | custom-call | flops 6442450944 | bytes 16777216 | tf_op jit(solution)/shard_map/pallas_call | solution.py:468
  116.1 1.1 copy.26
  (1 shorter events, 0.0 us)
Async XLA Ops:
  4.4 2.2 %copy-start = (bf16[512,4096]{1,0:T(8,128)(2,1)S(1)}, bf16[512,4096]{1,0:T(8,128)(2,1)}, u32[]{:S(2)}) copy-start(bf16[512,4096]{1,0:T(8,128)(2,1)} %embed.1) | copy-start | bytes 12582916
  4.5 2.1 %copy-start.1 = (f32[4096]{0:T(1024)S(1)}, f32[4096]{0:T(1024)}, u32[]{:S(2)}) copy-start(f32[4096]{0:T(1024)} %param.16) | copy-start | bytes 49156
  6.6 39.0 %copy-start.4 = (f32[128,1024]{1,0:T(8,128)S(1)}, f32[128,1024]{1,0:T(8,128)}, u32[]{:S(2)}) copy-start(f32[128,1024]{1,0:T(8,128)} %filt_ref.1) | copy-start | bytes 1572868
  6.6 39.0 %copy-start.5 = (bf16[256,1024]{1,0:T(8,128)(2,1)S(1)}, bf16[256,1024]{1,0:T(8,128)(2,1)}, u32[]{:S(2)}) copy-start(bf16[256,1024]{1,0:T(8,128)(2,1)} %param.21) | copy-start | bytes 1572868
  6.6 39.0 %copy-start.6 = (f32[3,3,1024]{2,1,0:T(4,128)S(1)}, f32[3,3,1024]{2,1,0:T(4,128)}, u32[]{:S(2)}) copy-start(f32[3,3,1024]{2,1,0:T(4,128)} %short_ref.1) | copy-start | bytes 110596
  6.6 39.0 %copy-start.7 = (f32[1024]{0:T(1024)S(1)}, f32[1024]{0:T(1024)}, u32[]{:S(2)}) copy-start(f32[1024]{0:T(1024)} %param.20) | copy-start | bytes 12292
  43.5 1.7 %copy-start.2 = (bf16[32,96,512]{2,1,0:T(8,128)(2,1)}, bf16[32,96,512]{2,1,0:T(8,128)(2,1)S(1)}, u32[]{:S(2)}) copy-start(bf16[32,96,512]{2,1,0:T(8,128)(2,1)S(1)} %get-tuple-element.9.table_in) | copy-start | bytes 9437188
  45.6 1.9 %copy-start.3 = (bf16[32,96,512]{2,1,0:T(8,128)(2,1)S(1)}, bf16[32,96,512]{2,1,0:T(8,128)(2,1)}, u32[]{:S(2)}) copy-start(bf16[32,96,512]{2,1,0:T(8,128)(2,1)} %copy-done.2) | copy-start | bytes 9437188
